TPU v7x, 512 devices: a whole 4x4x16 slice. The times are simulated.
512 devices in a mesh: pair: 64 (over z, x_lo, core), spin: 8 (over y, x_hi).
Axes of the slice: x: 4 (x_hi: 2, x_lo: 2; x = x_hi * 2 + x_lo), y: 4, z: 16, core: 2. Of those that a mesh axis runs over, the one named last changes fastest.
Arguments:
- integrals: bfloat16 [4, 6144, 6144], P(None, 'pair'), may hold values from -6 to 6
- coef: bfloat16 [4, 6144, 384], P(None, 'pair', 'spin'), may hold values from -0.078125 to 0.078125
- live: int32 [64], replicated, may hold values from 1 to 96, 4608 in all
Outputs:
- transformed: float32 [2, 4, 768, 768], P(None, None, 'spin', 'pair')
Inputs may be any that keep to these rules, and one draw needn't show every extreme that they name: Some pair batch has all 96 functions live.
All inputs are finite; a program needn't handle non-finite values.
Results may differ from a plain program's by a relative error of at most 0.0029.
Values may be sent and summed in bfloat16 or wider, within the bound.
No kernel may reach another device: no remote copies, remote signals or barrier semaphores. Data moves between devices by JAX's collectives and lax.ppermute only.
A program may use at most 64 MiB of HBM per device.

v0:
```python
import jax
import jax.numpy as jnp
from jax import lax
from jax.sharding import PartitionSpec as P


def with_partners(block):
    bar = jnp.stack([-block[2], block[3], block[0], -block[1]])
    return jnp.concatenate([block, bar], axis=2)


def shards(integrals, coef, live):
    count_pq = integrals.shape[0]
    s_local = integrals.shape[1]
    here = lax.axis_index("pair")
    keep = jnp.arange(s_local, dtype=jnp.int32) < live[here]
    masked = jnp.where(keep[None, :, None], integrals, jnp.zeros((), jnp.bfloat16))
    flat_rows = masked.reshape(count_pq * s_local, masked.shape[2])
    local_full = with_partners(coef)
    k_block = local_full.shape[2]
    carry = lax.dot_general(
        lax.all_gather(local_full, "pair", axis=1, tiled=True),
        flat_rows,
        (((1,), (1,)), ((), ())),
        preferred_element_type=jnp.float32,
    )
    half = carry.astype(jnp.bfloat16).reshape(4, k_block, count_pq, s_local)
    columns = half.transpose(0, 3, 1, 2).reshape(4 * s_local, k_block * count_pq)
    row_coef = lax.all_gather(local_full, "spin", axis=2, tiled=True)
    spinors = row_coef.shape[2]
    w_real = row_coef.reshape(4 * s_local, spinors)
    w_imag = jnp.stack([row_coef[1], -row_coef[0], row_coef[3], -row_coef[2]]).reshape(
        4 * s_local, spinors
    )
    dims = (((0,), (0,)), ((), ()))
    groups = lax.axis_size("pair")
    l_block = spinors // groups
    term_real = lax.dot_general(w_real, columns, dims, preferred_element_type=jnp.float32)
    term_imag = lax.dot_general(w_imag, columns, dims, preferred_element_type=jnp.float32)
    summed = lax.psum_scatter(
        jnp.concatenate([term_real, term_imag], axis=1), "pair", scatter_dimension=0, tiled=True
    )
    result = summed.reshape(l_block, 2, k_block, count_pq).transpose(1, 3, 2, 0)
    return result


def solution(mesh):
    placed = (P(None, "pair", None), P(None, "pair", "spin"), P())
    return jax.shard_map(
        shards, mesh=mesh, in_specs=placed, out_specs=P(None, None, "spin", "pair"), check_vma=False
    )
```

profile of v0, /device:TPU:4, one launch (start us, length us, event | category | flops | bytes accessed | tf_op | source)
XLA Modules:
  0.0 597.2 jit_solution(6752907929978806606)
XLA Ops:
  6.5 0.0 all-gather.2.cloned.1.call-start
  6.5 0.8 copy.22
  7.4 0.1 slice_negate_fusion.3
  7.5 0.2 maximum_maximum_fusion
  7.7 0.8 copy.24
  8.4 0.0 all-gather.2.cloned.1.call-update
  8.5 0.0 all-reduce.3.cloned.1.call-start
  8.5 39.3 %all_gather.6 = bf16[4,96,768]{1,0,2:T(4,128)(2,1)S(1)} all-gather(bf16[4,96,96]{1,0,2:T(4,128)(2,1)S(1)} %maximum_maximum_fusion), channel_id=1, replica_groups=mesh['pair'=64,'spin'=8] {'spin'}, dimensions={2}, use_global_device_ids=true | all-gather | bytes 663552 | tf_op jit(solution)/shard_map/all_gather | solution.py:29
  47.8 0.6 copy.23
  48.4 1.2 dynamic_slice.3
  49.7 0.7 iota_compare_fusion
  50.4 0.1 pad_maximum_fusion.1
  50.4 4.9 broadcast_select_fusion
  55.4 85.5 %all-gather.2.cloned.1.call-done = bf16[4,6144,96]{2,0,1:T(4,128)(2,1)} async-done(((bf16[4,96,96]{2,0,1:T(4,128)(2,1)}), bf16[4,6144,96]{2,0,1:T(4,128)(2,1)}) %all-gather.2.cloned.1.call-update) | async-done | bytes 4718608 | tf_op jit(solution)/shard_map/all_gather | solution.py:22
  140.9 7.6 %fusion.2 = bf16[4,96,384]{2,1,0:T(8,128)(2,1)S(1)} fusion(bf16[384,6144,1]{1,0,2:T(8,128)(2,1)} %bitcast.22, bf16[4,6144,96]{2,0,1:T(4,128)(2,1)} %all-gather.2.cloned.1.call-done), kind=kOutput, calls=%fused_computation.4 | convolution fusion | flops 1812086784 | bytes 9732096 | tf_op jit(solution)/shard_map/dot_general | solution.py:21
  148.5 0.3 reshape.24
  148.7 0.5 copy.39
  149.2 0.3 reshape.25
  149.5 0.5 fusion.7
  150.0 0.5 fusion.6
  150.5 1.6 pad_maximum_fusion
  152.0 0.0 all-reduce.3.cloned.1.call-update
  152.1 1.3 dynamic-slice
  154.0 434.3 %all-reduce.3.cloned.1.call-done = f32[768,768]{0,1:T(8,128)} async-done(((f32[768,768]{0,1:T(8,128)}), f32[768,768]{0,1:T(8,128)}) %all-reduce.3.cloned.1.call-update) | async-done | bytes 2359312
  588.3 1.3 constant_dynamic-slice_fusion
  589.6 0.8 copy.31
  (1 shorter events, 0.0 us)
Async XLA Ops:
  6.5 134.3 %all-gather.2.cloned.1.call-start = ((), (), s32[]{:S(2)}) async-start(), calls=%async_computation | async-start | bytes 6389760 | tf_op jit(solution)/shard_map/all_gather | solution.py:22
  8.5 579.8 %all-reduce.3.cloned.1.call-start = ((), (), s32[]{:S(2)}) async-start(), calls=%async_computation.1 | async-start | bytes 4718592
Sparse Core Ops, SparseCore 0:
  9.5 131.3 all-gather.1
  152.2 436.0 all-reduce.2
where the time goes:
time: 597 us
  waiting for transfers between devices  520 us (87%)
  blocking collectives  39.3 us (7%)
  between operations  14.1 us (2%)
  matrix products  8.53 us (1%)
  local copies, waits for them, and re-layouts  7.8 us (1%)
  other arithmetic  7.56 us (1%)
    unnamed x3, waiting for transfers between devices  434 us
    all_gather x1, waiting for transfers between devices, shards(): lax.all_gather(local_full, 'pair', axis=1, tiled=True)  85.5 us
    all_gather x1, blocking collectives, shards(): row_coef = lax.all_gather(local_full, 'spin', axis=2, tiled=True)  39.3 us
  transfers between devices with their start and end apart: 2, of which 2 were waited for; matrix products, arithmetic and copies ran while one was open for 1% of the time, Pallas kernels for 0%

commit v1 on v0

v1 whole, which is shorter than its diff:
```python
import jax
import jax.numpy as jnp
import numpy as np
from jax import lax
from jax.experimental import pallas as pl
from jax.experimental.pallas import tpu as pltpu
from jax.sharding import PartitionSpec as P

S, K, PQ, PLANES, Q, SPIN = 96, 48, 4, 16, 4, 8
J = K // Q
PLANE = Q * S
CK = 4 * K
PACKED = CK * S // 128

NEAR = [[4 * (4 * h + l) + q for l in range(4)] for h in range(4) for q in range(Q)]
FAR = [[4 * (4 * h + l) + q for h in range(4)] for l in range(4) for q in range(Q)]
LINE = [[4 * z + q for z in range(PLANES)] for q in range(Q)]
PLANE_GROUP = [[4 * z + q for q in range(Q)] for z in range(PLANES)]


def swap(bit):
    return [(i, i ^ bit) for i in range(Q * PLANES)]


def signs():
    table = (
        ((0, 1), (1, 1), (2, 1), (3, 1)),
        ((1, 1), (0, -1), (3, 1), (2, -1)),
        ((2, -1), (3, 1), (0, 1), (1, -1)),
        ((3, 1), (2, 1), (1, -1), (0, -1)),
    )
    out = np.zeros((4, 4, J, 4, J), np.float32)
    for v, row in enumerate(table):
        for c, (source, sign) in enumerate(row):
            for j in range(J):
                out[c, v, j, source, j] = sign
    return out.reshape(CK, 4 * J)


def nt(a, b):
    return lax.dot_general(a, b, (((1,), (1,)), ((), ())), preferred_element_type=jnp.float32)


def pack_kernel(coef_ref, out_ref):
    full = coef_ref[...].reshape(CK, S)
    tail = full[PACKED:]
    side = jnp.concatenate([tail[:, 32 * i : 32 * i + 32] for i in range(3)], axis=0)
    out_ref[...] = jnp.concatenate([full[:PACKED], side], axis=1)


def unpack(block):
    side = block[:, S:]
    tail = jnp.concatenate([side[K * i : K * i + K] for i in range(3)], axis=1)
    return jnp.concatenate([block[:, :S], tail], axis=0)


def half_kernel(live_ref, own_ref, other_ref, integrals_ref, half_ref, rows_ref, total_ref, plane_ref):
    step = pl.program_id(0)
    here = lax.axis_index("pair")
    z, q = here // Q, here % Q
    x, core = q // 2, q % 2

    @pl.when(step == 0)
    def _():
        total_ref[...] = jnp.zeros_like(total_ref)

    total = total_ref[...]
    for near in range(4):
        slot = near * 4 + step
        blocks = []
        for place in range(Q):
            column = (place // 2) ^ x
            mine, theirs = own_ref[column, slot], other_ref[column, slot]
            blocks.append(unpack(jnp.where(core == place % 2, mine, theirs)))
        plane = jnp.concatenate(blocks, axis=1)

        @pl.when(z == step * 4 + near)
        def _():
            plane_ref[...] = plane

        part = integrals_ref[:, :, near * PLANE : (near + 1) * PLANE].reshape(PQ * S, PLANE)
        total = total + nt(plane, part)
    total_ref[...] = total

    @pl.when(step == 3)
    def _():
        keep = lax.broadcasted_iota(jnp.int32, (CK, S), 1) < live_ref[here]
        for pq in range(PQ):
            part = jnp.where(keep, total[:, pq * S : (pq + 1) * S], 0.0)
            row = jnp.concatenate([part[c * K : (c + 1) * K] for c in range(4)], axis=1)
            half_ref[pq * K : (pq + 1) * K, :] = row.astype(jnp.bfloat16)
        row = lax.broadcasted_iota(jnp.int32, (4 * J, CK), 0)
        component = sum((row >= J * c).astype(jnp.int32) for c in range(1, 4))
        wanted = (K - J) * component + row + J * q
        pick = (lax.broadcasted_iota(jnp.int32, (4 * J, CK), 1) == wanted).astype(jnp.bfloat16)
        rows = jnp.dot(pick, plane_ref[...], preferred_element_type=jnp.float32).astype(jnp.bfloat16)
        for e in range(SPIN):
            rows_ref[e] = rows


def term_kernel(half_ref, rows_ref, signs_ref, out_ref):
    by_component = [
        jnp.concatenate([half_ref[place, :, c * S : (c + 1) * S] for place in range(Q)], axis=1) for c in range(4)
    ]
    half = jnp.concatenate(by_component, axis=1)
    weights = []
    for e in range(SPIN):
        signed = jnp.dot(signs_ref[...], rows_ref[e], preferred_element_type=jnp.float32).astype(jnp.bfloat16)
        weights.append(jnp.concatenate([signed[c * 4 * J : (c + 1) * 4 * J] for c in range(4)], axis=1))
    term = nt(jnp.concatenate(weights, axis=0), half)
    for e in range(SPIN):
        part = term[e * 4 * J : (e + 1) * 4 * J]
        side = jnp.concatenate([part[: 2 * J, 128:], part[2 * J :, 128:]], axis=1)
        block = jnp.concatenate([part[:, :128], side], axis=0).astype(jnp.bfloat16)
        out_ref[2 * e] = block
        out_ref[2 * e + 1] = block


def sum_kernel(terms_ref, out_ref):
    total = terms_ref[0].astype(jnp.float32)
    for z in range(1, PLANES):
        total = total + terms_ref[z].astype(jnp.float32)
    side = total[4 * J :]
    full = jnp.concatenate([total[: 4 * J], jnp.concatenate([side[:, :64], side[:, 64:]], axis=0)], axis=1)
    real, imag, real_bar, imag_bar = (full[v * J : (v + 1) * J] for v in range(4))
    barred = (lax.axis_index("pair") // Q) % 2 == 1
    parts = (
        (jnp.where(barred, real_bar, real), jnp.where(barred, real, -real_bar)),
        (jnp.where(barred, imag_bar, imag), jnp.where(barred, -imag, imag_bar)),
    )
    for t, (unbarred, partner) in enumerate(parts):
        for pq in range(PQ):
            columns = slice(pq * K, (pq + 1) * K)
            out_ref[t, :, pq, :] = jnp.concatenate([unbarred[:, columns], partner[:, columns]], axis=1)


def shards(integrals, coef, live):
    bf16 = jnp.bfloat16
    vmem = pl.BlockSpec(memory_space=pltpu.VMEM)
    limit = pltpu.CompilerParams(vmem_limit_bytes=48 * 1024 * 1024)
    packed = pl.pallas_call(
        pack_kernel,
        out_shape=jax.ShapeDtypeStruct((PACKED, 128), bf16),
        in_specs=[vmem],
        out_specs=vmem,
        compiler_params=limit,
    )(coef.transpose(0, 2, 1))
    line = lax.all_gather(packed, "pair", axis_index_groups=FAR, tiled=True)
    line = lax.all_gather(line, "pair", axis_index_groups=NEAR, tiled=True)
    own = jnp.concatenate([line, lax.ppermute(line, "pair", swap(2))])
    other = lax.ppermute(own, "pair", swap(1))
    half, rows = pl.pallas_call(
        half_kernel,
        grid=(4,),
        out_shape=(
            jax.ShapeDtypeStruct((PQ * K, 4 * S), bf16),
            jax.ShapeDtypeStruct((SPIN, 4 * J, PLANE), bf16),
        ),
        in_specs=[
            pl.BlockSpec(memory_space=pltpu.SMEM),
            vmem,
            vmem,
            pl.BlockSpec((PQ, S, 4 * PLANE), lambda i: (0, 0, i)),
        ],
        out_specs=(vmem, vmem),
        scratch_shapes=[pltpu.VMEM((CK, PQ * S), jnp.float32), pltpu.VMEM((CK, PLANE), bf16)],
        compiler_params=limit,
    )(live, own.reshape(2, PLANES, PACKED, 128), other.reshape(2, PLANES, PACKED, 128), integrals)
    rows = lax.all_to_all(rows, "spin", 0, 0)
    halves = lax.all_gather(half, "pair", axis_index_groups=PLANE_GROUP)
    terms = pl.pallas_call(
        term_kernel,
        out_shape=jax.ShapeDtypeStruct((PLANES, 72, 128), bf16),
        in_specs=[vmem] * 3,
        out_specs=vmem,
        compiler_params=limit,
    )(halves, rows, jnp.asarray(signs(), bf16))
    terms = lax.all_to_all(terms, "pair", 0, 0, axis_index_groups=LINE)
    out = pl.pallas_call(
        sum_kernel,
        out_shape=jax.ShapeDtypeStruct((2, J, PQ, 2 * K), jnp.float32),
        in_specs=[vmem],
        out_specs=vmem,
        compiler_params=limit,
    )(terms)
    return out.transpose(0, 2, 3, 1)


def solution(mesh):
    placed = (P(None, "pair", None), P(None, "pair", "spin"), P())
    return jax.shard_map(
        shards, mesh=mesh, in_specs=placed, out_specs=P(None, None, "spin", "pair"), check_vma=False
    )
```

time: 597 us -> 112 us (0.19)
  waiting for transfers between devices: 520 us -> 11.4 us
  blocking collectives: 39.3 us -> 77.1 us
  between operations: 14.1 us -> 0.04 us
  starting transfers between devices: 0.04 us -> 12.7 us
  Pallas kernels: 0 us -> 9.21 us
  matrix products: 8.53 us -> 0 us
  other arithmetic: 7.56 us -> 0 us
  local copies, waits for them, and re-layouts: 7.8 us -> 0.92 us
    unnamed x3 -> x0, waiting for transfers between devices: 434 us -> none
    all_gather x1 -> x0, waiting for transfers between devices: 85.5 us -> none  [shards(): lax.all_gather(local_full, 'pair', axis=1, tiled=True)]
    all_to_all x0 -> x1, blocking collectives: none -> 26.6 us  [shards(): terms = lax.all_to_all(terms, 'pair', 0, 0, axis_index_groups=LINE)]
    ppermute x0 -> x2, waiting for transfers between devices: none -> 11.4 us  [the longest x1 8.62 us: shards(): own = jnp.concatenate([line, lax.ppermute(line, 'pair', swap(2))])]
    all_gather x1 -> x3, blocking collectives: 39.3 us -> 50.4 us  [the longest x1 25.9 us: shards(): line = lax.all_gather(packed, 'pair', axis_index_groups=FAR, tiled=True)]
    pallas_call x0 -> x4, Pallas kernels: none -> 9.21 us  [the longest x1 7.41 us: shards(): pl.pallas_call(half_kernel, grid=(4,), out_shape=(jax.ShapeDtypeStruct((P...]
    dot_general x3 -> x0, matrix products: 8.53 us -> none  [the longest x1 7.6 us: shards(): lax.dot_general(lax.all_gather(local_full, 'pair', axis=1, tiled=True), f...]
    all_to_all x0 -> x1, starting transfers between devices: none -> 7.56 us  [shards(): rows = lax.all_to_all(rows, 'spin', 0, 0)]
  transfers between devices with their start and end apart: 2 -> 3, of which waited for: 2 -> 2; matrix products, arithmetic and copies ran while one was open for 1% -> 0% of each run, Pallas kernels for 0% -> 0%
where the time goes in v1:
time: 112 us; the launch traced here: 111 us
  blocking collectives  77.1 us (69%)
  starting transfers between devices  12.7 us (11%)
  waiting for transfers between devices  11.4 us (10%)
  Pallas kernels  9.21 us (8%)
    all_to_all x1, blocking collectives, shards(): terms = lax.all_to_all(terms, 'pair', 0, 0, axis_index_groups=LINE)  26.6 us
    all_gather x1, blocking collectives, shards(): line = lax.all_gather(packed, 'pair', axis_index_groups=FAR, tiled=True)  25.9 us
    all_gather x1, blocking collectives, shards(): line = lax.all_gather(line, 'pair', axis_index_groups=NEAR, tiled=True)  15.5 us
    all_gather x1, blocking collectives, shards(): halves = lax.all_gather(half, 'pair', axis_index_groups=PLANE_GROUP)  9.02 us
    ppermute x1, waiting for transfers between devices, shards(): own = jnp.concatenate([line, lax.ppermute(line, 'pair', swap(2))])  8.62 us
    all_to_all x1, starting transfers between devices, shards(): rows = lax.all_to_all(rows, 'spin', 0, 0)  7.56 us
    pallas_call x1, Pallas kernels, shards(): pl.pallas_call(half_kernel, grid=(4,), out_shape=(jax.ShapeDtypeStruct((P...  7.41 us
    ppermute x1, starting transfers between devices, shards(): own = jnp.concatenate([line, lax.ppermute(line, 'pair', swap(2))])  3.23 us
  transfers between devices with their start and end apart: 3, of which 2 were waited for; matrix products, arithmetic and copies ran while one was open for 0% of the time, Pallas kernels for 0%

profile of v1, /device:TPU:4, one launch (start us, length us, event | category | flops | bytes accessed | tf_op | source)
XLA Modules:
  0.0 111.4 jit_solution(10553638247751850352)
XLA Ops:
  0.0 0.0 copy-start.1
  0.0 0.8 copy-done.1
  0.8 0.1 shard_map.46
  0.9 25.9 %all_gather.12 = bf16[576,128]{1,0:T(8,128)(2,1)S(1)} all-gather(bf16[144,128]{1,0:T(8,128)(2,1)S(1)} %shard_map.46), channel_id=1, replica_groups={{0,128,256,384},{8,136,264,392},{16,144,272,400},{24,152,280,408},{32,1..., dimensions={0}, use_global_device_ids=true | all-gather | bytes 184320 | tf_op jit(solution)/shard_map/all_gather | solution.py:148
  26.8 15.5 %all_gather.13 = bf16[2304,128]{1,0:T(8,128)(2,1)S(1)} all-gather(bf16[576,128]{1,0:T(8,128)(2,1)S(1)} %all_gather.12), channel_id=1, replica_groups={{0,32,64,96},{8,40,72,104},{16,48,80,112},{24,56,88,120},{128,160,192,2..., dimensions={0}, use_global_device_ids=true | all-gather | bytes 737280 | tf_op jit(solution)/shard_map/all_gather | solution.py:149
  42.4 0.0 copy-start.2
  42.4 3.2 %collective-permute-start = (bf16[2304,128]{1,0:T(8,128)(2,1)S(1)}, bf16[2304,128]{1,0:T(8,128)(2,1)S(1)}, u32[]{:S(2)}, u32[]{:S(2)}) collective-permute-start(bf16[2304,128]{1,0:T(8,128)(2,1)S(1)} %all_gather.13), channel_id=1, source_target_pairs={{0,16},{8,24},{16,0},{24,8},{32,48},{40,56},{48,32},{56,40},{64,80... | collective-permute-start | bytes 1769480 | tf_op jit(solution)/shard_map/ppermute | solution.py:150
  45.6 8.6 %collective-permute-done = bf16[2304,128]{1,0:T(8,128)(2,1)S(1)} collective-permute-done((bf16[2304,128]{1,0:T(8,128)(2,1)S(1)}, bf16[2304,128]{1,0:T(8,128)(2,1)S(1)}, u32[]{:S(2)}, u32[]{:S(2)}) %collective-permute-start) | collective-permute-done | bytes 589856 | tf_op jit(solution)/shard_map/ppermute | solution.py:150
  54.3 0.1 constant_dynamic-update-slice_fusion
  54.3 1.9 %collective-permute-start.1 = (bf16[4608,128]{1,0:T(8,128)(2,1)S(1)}, bf16[4608,128]{1,0:T(8,128)(2,1)S(1)}, u32[]{:S(2)}, u32[]{:S(2)}) collective-permute-start(bf16[4608,128]{1,0:T(8,128)(2,1)S(1)} %constant_dynamic-update-slice_fusion), channel_id=1, source_target_pairs={{0,8},{8,0},{16,24},{24,16},{32,40},{40,32},{48,56},{56,48},{64,72... | collective-permute-start | bytes 3538952 | tf_op jit(solution)/shard_map/ppermute | solution.py:151
  56.3 2.8 %collective-permute-done.1 = bf16[4608,128]{1,0:T(8,128)(2,1)S(1)} collective-permute-done((bf16[4608,128]{1,0:T(8,128)(2,1)S(1)}, bf16[4608,128]{1,0:T(8,128)(2,1)S(1)}, u32[]{:S(2)}, u32[]{:S(2)}) %collective-permute-start.1) | collective-permute-done | bytes 1179680 | tf_op jit(solution)/shard_map/ppermute | solution.py:151
  59.1 0.0 copy-done.2
  59.1 7.4 %shard_map.47 = (bf16[192,384]{1,0:T(8,128)(2,1)S(1)}, bf16[8,48,384]{2,1,0:T(8,128)(2,1)}) custom-call(s32[64]{0:T(128)S(1)} %copy-done.2, bf16[2,16,144,128]{3,2,1,0:T(8,128)(2,1)S(1)} %bitcast.5, bf16[2,16,144,128]{3,2,1,0:T(8,128)(2,1)S(1)} %bitcast.7, bf16[4,96,6144]{2,1,0:T(8,128)(2,1)} %integrals_ref.1), custom_call_target="tpu_custom_call" | custom-call | tf_op jit(solution)/shard_map/pallas_call | solution.py:152
  66.5 0.0 copy-start
  66.5 7.6 %all-to-all-start = ((bf16[8,48,384]{2,1,0:T(8,128)(2,1)}), bf16[8,48,384]{2,1,0:T(8,128)(2,1)S(1)}, u32[]{:S(2)}, u32[]{:S(2)}) async-start(bf16[8,48,384]{2,1,0:T(8,128)(2,1)} %get-tuple-element.8), calls=%async_computation | async-start | bytes 589824 | tf_op jit(solution)/shard_map/all_to_all | solution.py:169
  74.1 9.0 %all-gather = bf16[768,384]{1,0:T(8,128)(2,1)S(1)} all-gather(bf16[192,384]{1,0:T(8,128)(2,1)S(1)} %get-tuple-element.7), channel_id=2, replica_groups={{0,8,16,24},{32,40,48,56},{64,72,80,88},{96,104,112,120},{128,136,144,1..., dimensions={0}, use_global_device_ids=true | all-gather | bytes 737280 | tf_op jit(solution)/shard_map/all_gather | solution.py:170
  83.1 0.0 all-to-all-done.rows_ref
  83.1 0.0 copy-done
  83.1 0.9 shard_map.48
  83.9 26.6 %all_to_all.10.terms_ref = bf16[16,72,128]{2,1,0:T(8,128)(2,1)S(1)} all-to-all(bf16[16,72,128]{2,1,0:T(8,128)(2,1)S(1)} %shard_map.48), channel_id=1, replica_groups={{0,32,64,96,128,160,192,224,256,288,320,352,384,416,448,480},{8,40,72,1..., dimensions={0} | all-to-all | bytes 589824 | tf_op jit(solution)/shard_map/all_to_all | solution.py:178
  110.6 0.8 shard_map.49
  (1 shorter events, 0.0 us)
Async XLA Ops:
  0.0 0.8 copy-start.1
  42.4 16.7 %copy-start.2 = (s32[64]{0:T(128)S(1)}, s32[64]{0:T(128)}, u32[]{:S(2)}) copy-start(s32[64]{0:T(128)} %live_ref.1) | copy-start | bytes 772
  42.4 11.9 %collective-permute-start = (bf16[2304,128]{1,0:T(8,128)(2,1)S(1)}, bf16[2304,128]{1,0:T(8,128)(2,1)S(1)}, u32[]{:S(2)}, u32[]{:S(2)}) collective-permute-start(bf16[2304,128]{1,0:T(8,128)(2,1)S(1)} %all_gather.13), channel_id=1, source_target_pairs={{0,16},{8,24},{16,0},{24,8},{32,48},{40,56},{48,32},{56,40},{64,80... | collective-permute-start | bytes 1769480 | tf_op jit(solution)/shard_map/ppermute | solution.py:150
  54.3 4.7 %collective-permute-start.1 = (bf16[4608,128]{1,0:T(8,128)(2,1)S(1)}, bf16[4608,128]{1,0:T(8,128)(2,1)S(1)}, u32[]{:S(2)}, u32[]{:S(2)}) collective-permute-start(bf16[4608,128]{1,0:T(8,128)(2,1)S(1)} %constant_dynamic-update-slice_fusion), channel_id=1, source_target_pairs={{0,8},{8,0},{16,24},{24,16},{32,40},{40,32},{48,56},{56,48},{64,72... | collective-permute-start | bytes 3538952 | tf_op jit(solution)/shard_map/ppermute | solution.py:151
  66.5 16.6 %copy-start = (bf16[192,48]{1,0:T(8,128)(2,1)S(1)}, bf16[192,48]{1,0:T(8,128)(2,1)}, u32[]{:S(2)}) copy-start(bf16[192,48]{1,0:T(8,128)(2,1)} %constant.2.clone.signs_ref) | copy-start | bytes 55300
  66.5 16.6 %all-to-all-start = ((bf16[8,48,384]{2,1,0:T(8,128)(2,1)}), bf16[8,48,384]{2,1,0:T(8,128)(2,1)S(1)}, u32[]{:S(2)}, u32[]{:S(2)}) async-start(bf16[8,48,384]{2,1,0:T(8,128)(2,1)} %get-tuple-element.8), calls=%async_computation | async-start | bytes 589824 | tf_op jit(solution)/shard_map/all_to_all | solution.py:169

commit v2 on v1

v2 whole, which is shorter than its diff:
```python
import jax
import jax.numpy as jnp
import numpy as np
from jax import lax
from jax.experimental import pallas as pl
from jax.experimental.pallas import tpu as pltpu
from jax.sharding import PartitionSpec as P

S, K, PQ, PLANES, Q, SPIN = 96, 48, 4, 16, 4, 8
J = K // Q
PLANE = Q * S
CK = 4 * K
PACKED = CK * S // 128

FOLD = [0, 1, 3, 2]
NEAR = [[4 * (4 * h + l) + q for l in FOLD] for h in range(4) for q in range(Q)]
FAR = [[4 * (4 * h + l) + q for h in range(4)] for l in range(4) for q in range(Q)]
LINE = [[4 * z + q for z in range(PLANES)] for q in range(Q)]
CHIP = [[2 * i, 2 * i + 1] for i in range(Q * PLANES // 2)]


def swap(bit):
    return [(i, i ^ bit) for i in range(Q * PLANES)]


def signs():
    table = (
        ((0, 1), (1, 1), (2, 1), (3, 1)),
        ((1, 1), (0, -1), (3, 1), (2, -1)),
        ((2, -1), (3, 1), (0, 1), (1, -1)),
        ((3, 1), (2, 1), (1, -1), (0, -1)),
    )
    out = np.zeros((4, 4, J, 4, J), np.float32)
    for v, row in enumerate(table):
        for c, (source, sign) in enumerate(row):
            for j in range(J):
                out[c, v, j, source, j] = sign
    return out.reshape(CK, 4 * J)


def nt(a, b):
    return lax.dot_general(a, b, (((1,), (1,)), ((), ())), preferred_element_type=jnp.float32)


def turn(x, lanes):
    return x if lanes == 0 else jnp.concatenate([x[:, 128 - lanes :], x[:, : 128 - lanes]], axis=1)


def pack_kernel(coef_ref, out_ref):
    q = lax.axis_index("pair") % Q
    full = coef_ref[...].reshape(CK, S)
    tail = full[PACKED:]
    side = jnp.concatenate([tail[:, 32 * i : 32 * i + 32] for i in range(3)], axis=0)
    packed = jnp.concatenate([full[:PACKED], side], axis=1)
    turned = packed
    for place in range(1, Q):
        turned = jnp.where(q == place, turn(packed, S * place % 128), turned)
    out_ref[...] = turned


def plane_of(blocks, lane):
    p0, p1, p2, p3 = blocks
    main = [jnp.where(lane < 96, p0, p1), jnp.where(lane < 64, p1, p2), jnp.where(lane < 32, p2, p3)]
    side = jnp.where(lane < 32, p3, jnp.where(lane < 64, p2, jnp.where(lane < 96, p1, p0)))
    turned = [turn(side[K * i : K * i + K], 32 * (i + 1)) for i in range(3)]
    low = lane[:K]
    tail = [
        jnp.where((low >= 32) & (low < 64), turned[(t + 1) % 3], jnp.where((low >= 64) & (low < 96), turned[(t + 2) % 3], turned[t]))
        for t in range(3)
    ]
    return jnp.concatenate([jnp.concatenate(main, axis=1), jnp.concatenate(tail, axis=1)], axis=0)


def half_kernel(live_ref, own_ref, other_ref, integrals_ref, half_ref):
    here = lax.axis_index("pair")
    x, core = here % Q // 2, here % 2
    lane = lax.broadcasted_iota(jnp.int32, (PACKED, 128), 1)
    total = None
    for h in range(4):
        planes = []
        for l in range(4):
            slot = FOLD.index(l) * 4 + h
            blocks = []
            for place in range(Q):
                column = (place // 2) ^ x
                blocks.append(jnp.where(core == place % 2, own_ref[column, slot], other_ref[column, slot]))
            planes.append(plane_of(blocks, lane))
        part = integrals_ref[:, :, h * 4 * PLANE : (h + 1) * 4 * PLANE].reshape(PQ * S, 4 * PLANE)
        term = nt(jnp.concatenate(planes, axis=1), part)
        total = term if total is None else total + term
    keep = lax.broadcasted_iota(jnp.int32, (CK, S), 1) < live_ref[here]
    for pq in range(PQ):
        part = jnp.where(keep, total[:, pq * S : (pq + 1) * S], 0.0)
        row = jnp.concatenate([part[c * K : (c + 1) * K] for c in range(4)], axis=1)
        half_ref[pq * K : (pq + 1) * K, :] = row.astype(jnp.bfloat16)


def rows_kernel(coef_ref, out_ref):
    core = lax.axis_index("pair") % 2
    row = lax.broadcasted_iota(jnp.int32, (8 * J, CK), 0)
    x = (row >= 4 * J).astype(jnp.int32)
    row = row - 4 * J * x
    component = sum((row >= J * c).astype(jnp.int32) for c in range(1, 4))
    wanted = (K - J) * component + row + J * (2 * x + core)
    pick = (lax.broadcasted_iota(jnp.int32, (8 * J, CK), 1) == wanted).astype(jnp.bfloat16)
    picked = [jnp.dot(pick, coef_ref[c], preferred_element_type=jnp.float32) for c in range(2)]
    rows = jnp.concatenate(picked, axis=1).astype(jnp.bfloat16)
    for e in range(SPIN):
        out_ref[e] = rows


def term_kernel(half_ref, rows_ref, signs_ref, own_ref, other_ref):
    x = lax.axis_index("pair") % Q // 2
    half = [jnp.concatenate([half_ref[core, :, c * S : (c + 1) * S] for core in range(2)], axis=1) for c in range(4)]
    terms = []
    for column in range(2):
        signed = [
            jnp.dot(signs_ref[...], rows_ref[e, 4 * J * column : 4 * J * (column + 1)], preferred_element_type=jnp.float32)
            for e in range(SPIN)
        ]
        term = None
        for c in range(4):
            weights = jnp.concatenate([part[4 * J * c : 4 * J * (c + 1)] for part in signed], axis=0)
            more = nt(weights.astype(jnp.bfloat16), half[c])
            term = more if term is None else term + more
        terms.append(term)
    own = jnp.where(x == 0, terms[0], terms[1])
    other = jnp.where(x == 0, terms[1], terms[0])
    for term, ref in ((own, own_ref), (other, other_ref)):
        for e in range(SPIN):
            part = term[e * 4 * J : (e + 1) * 4 * J]
            side = jnp.concatenate([part[: 2 * J, 128:], part[2 * J :, 128:]], axis=1)
            ref[e] = jnp.concatenate([part[:, :128], side], axis=0).astype(ref.dtype)


def join_kernel(own_ref, other_ref, out_ref):
    for e in range(SPIN):
        block = (own_ref[e] + other_ref[e].astype(jnp.float32)).astype(jnp.bfloat16)
        out_ref[2 * e] = block
        out_ref[2 * e + 1] = block


def sum_kernel(terms_ref, out_ref):
    total = terms_ref[0].astype(jnp.float32)
    for z in range(1, PLANES):
        total = total + terms_ref[z].astype(jnp.float32)
    side = total[4 * J :]
    full = jnp.concatenate([total[: 4 * J], jnp.concatenate([side[:, :64], side[:, 64:]], axis=0)], axis=1)
    real, imag, real_bar, imag_bar = (full[v * J : (v + 1) * J] for v in range(4))
    barred = (lax.axis_index("pair") // Q) % 2 == 1
    parts = (
        (jnp.where(barred, real_bar, real), jnp.where(barred, real, -real_bar)),
        (jnp.where(barred, imag_bar, imag), jnp.where(barred, -imag, imag_bar)),
    )
    for t, (unbarred, partner) in enumerate(parts):
        for pq in range(PQ):
            columns = slice(pq * K, (pq + 1) * K)
            out_ref[t, :, pq, :] = jnp.concatenate([unbarred[:, columns], partner[:, columns]], axis=1)


def call(kernel, out_shape, in_specs=None, mib=16):
    vmem = pl.BlockSpec(memory_space=pltpu.VMEM)

    def run(*args):
        return pl.pallas_call(
            kernel,
            out_shape=out_shape,
            in_specs=in_specs or [vmem] * len(args),
            out_specs=jax.tree.map(lambda _: vmem, out_shape),
            compiler_params=pltpu.CompilerParams(vmem_limit_bytes=mib * 1024 * 1024),
        )(*args)

    return run


def shards(integrals, coef, live):
    bf16 = jnp.bfloat16
    shape = jax.ShapeDtypeStruct
    vmem = pl.BlockSpec(memory_space=pltpu.VMEM)
    coef = coef.transpose(0, 2, 1)
    packed = call(pack_kernel, shape((PACKED, 128), bf16))(coef)
    line = lax.all_gather(packed, "pair", axis_index_groups=FAR, tiled=True)
    line = lax.all_gather(line, "pair", axis_index_groups=NEAR, tiled=True)
    line, coef = lax.optimization_barrier((line, coef))
    own = jnp.concatenate([line, lax.ppermute(line, "pair", swap(2))])

    pairs = lax.all_gather(coef.reshape(CK, S), "pair", axis_index_groups=CHIP)
    rows = call(rows_kernel, shape((SPIN, 8 * J, 2 * S), bf16))(pairs)
    rows = lax.all_to_all(rows, "spin", 0, 0)

    other = lax.ppermute(own, "pair", swap(1))
    half = call(
        half_kernel,
        shape((PQ * K, 4 * S), bf16),
        [pl.BlockSpec(memory_space=pltpu.SMEM), vmem, vmem, vmem],
        24,
    )(live, own.reshape(2, PLANES, PACKED, 128), other.reshape(2, PLANES, PACKED, 128), integrals)
    halves = lax.all_gather(half, "pair", axis_index_groups=CHIP)
    keep, give = call(
        term_kernel,
        (shape((SPIN, 72, 128), jnp.float32), shape((SPIN, 72, 128), bf16)),
    )(halves, rows, jnp.asarray(signs(), bf16))
    terms = call(join_kernel, shape((PLANES, 72, 128), bf16))(keep, lax.ppermute(give, "pair", swap(2)))
    terms = lax.all_to_all(terms, "pair", 0, 0, axis_index_groups=LINE)
    out = call(sum_kernel, shape((2, J, PQ, 2 * K), jnp.float32))(terms)
    return out.transpose(0, 2, 3, 1)


def solution(mesh):
    placed = (P(None, "pair", None), P(None, "pair", "spin"), P())
    return jax.shard_map(
        shards, mesh=mesh, in_specs=placed, out_specs=P(None, None, "spin", "pair"), check_vma=False
    )
```

time: 112 us -> 110 us (0.982)
  the two profiles are of different devices: /device:TPU:4 before, /device:TPU:32 now
where the time goes in v2:
time: 110 us
  blocking collectives  68.9 us (63%)
  waiting for transfers between devices  16.4 us (15%)
  starting transfers between devices  14.9 us (14%)
  Pallas kernels  6 us (5%)
  local copies, waits for them, and re-layouts  3.26 us (3%)
    all_gather x1, blocking collectives, shards(): line = lax.all_gather(packed, 'pair', axis_index_groups=FAR, tiled=True)  25 us
    all_to_all x1, blocking collectives, shards(): terms = lax.all_to_all(terms, 'pair', 0, 0, axis_index_groups=LINE)  25 us
    all_gather x1, blocking collectives, shards(): line = lax.all_gather(line, 'pair', axis_index_groups=NEAR, tiled=True)  14 us
    ppermute x1, waiting for transfers between devices, shards(): own = jnp.concatenate([line, lax.ppermute(line, 'pair', swap(2))])  8.31 us
    all_to_all x1, starting transfers between devices, shards(): rows = lax.all_to_all(rows, 'spin', 0, 0)  6.93 us
    pallas_call x6, Pallas kernels, run(): pl.pallas_call(kernel, out_shape=out_shape, in_specs=in_specs or [vmem] *...  6 us
    ppermute x1, waiting for transfers between devices, shards(): lax.ppermute(give, 'pair', swap(2))  4.53 us
    all_to_all x1, waiting for transfers between devices, shards(): rows = lax.all_to_all(rows, 'spin', 0, 0)  3.57 us
  transfers between devices with their start and end apart: 4, of which 3 were waited for; matrix products, arithmetic and copies ran while one was open for 0% of the time, Pallas kernels for 3%

profile of v2, /device:TPU:32, one launch (start us, length us, event | category | flops | bytes accessed | tf_op | source)
XLA Modules:
  0.0 109.5 jit_solution(1129673503365561738)
XLA Ops:
  0.0 0.0 copy-start.1
  0.0 0.8 copy-done.1
  0.8 0.2 shard_map.46
  1.0 25.0 %all_gather.15 = bf16[576,128]{1,0:T(8,128)(2,1)S(1)} all-gather(bf16[144,128]{1,0:T(8,128)(2,1)S(1)} %shard_map.46), channel_id=1, replica_groups={{0,128,256,384},{8,136,264,392},{16,144,272,400},{24,152,280,408},{32,1..., dimensions={0}, use_global_device_ids=true | all-gather | bytes 184320 | tf_op jit(solution)/shard_map/all_gather | solution.py:182
  26.0 14.0 %all_gather.16 = bf16[2304,128]{1,0:T(8,128)(2,1)S(1)} all-gather(bf16[576,128]{1,0:T(8,128)(2,1)S(1)} %all_gather.15), channel_id=1, replica_groups={{0,32,96,64},{8,40,104,72},{16,48,112,80},{24,56,120,88},{128,160,224,1..., dimensions={0}, use_global_device_ids=true | all-gather | bytes 737280 | tf_op jit(solution)/shard_map/all_gather | solution.py:183
  40.0 0.0 copy-start.2
  40.0 3.5 %collective-permute-start = (bf16[2304,128]{1,0:T(8,128)(2,1)S(1)}, bf16[2304,128]{1,0:T(8,128)(2,1)S(1)}, u32[]{:S(2)}, u32[]{:S(2)}) collective-permute-start(bf16[2304,128]{1,0:T(8,128)(2,1)S(1)} %all_gather.16), channel_id=1, source_target_pairs={{0,16},{8,24},{16,0},{24,8},{32,48},{40,56},{48,32},{56,40},{64,80... | collective-permute-start | bytes 1769480 | tf_op jit(solution)/shard_map/ppermute | solution.py:185
  43.6 0.0 copy-start.4
  43.6 8.3 %collective-permute-done = bf16[2304,128]{1,0:T(8,128)(2,1)S(1)} collective-permute-done((bf16[2304,128]{1,0:T(8,128)(2,1)S(1)}, bf16[2304,128]{1,0:T(8,128)(2,1)S(1)}, u32[]{:S(2)}, u32[]{:S(2)}) %collective-permute-start) | collective-permute-done | bytes 589856 | tf_op jit(solution)/shard_map/ppermute | solution.py:185
  51.9 0.1 constant_dynamic-update-slice_fusion
  52.0 1.9 %collective-permute-start.1 = (bf16[4608,128]{1,0:T(8,128)(2,1)S(1)}, bf16[4608,128]{1,0:T(8,128)(2,1)S(1)}, u32[]{:S(2)}, u32[]{:S(2)}) collective-permute-start(bf16[4608,128]{1,0:T(8,128)(2,1)S(1)} %constant_dynamic-update-slice_fusion), channel_id=1, source_target_pairs={{0,8},{8,0},{16,24},{24,16},{32,40},{40,32},{48,56},{56,48},{64,72... | collective-permute-start | bytes 3538952 | tf_op jit(solution)/shard_map/ppermute | solution.py:191
  53.9 0.0 copy-done.2
  53.9 2.9 %all_gather.19.coef_ref = bf16[2,192,96]{2,1,0:T(8,128)(2,1)S(1)} all-gather(bf16[1,192,96]{2,1,0:T(8,128)(2,1)S(1)} %bitcast.10), channel_id=1, replica_groups={{0,8},{16,24},{32,40},{48,56},{64,72},{80,88},{96,104},{112,120},{128,1..., dimensions={0}, use_global_device_ids=true | all-gather | bytes 110592 | tf_op jit(solution)/shard_map/all_gather | solution.py:187
  56.8 1.0 shard_map.48
  57.8 6.9 %all-to-all-start = ((bf16[8,96,192]{2,1,0:T(8,128)(2,1)}), bf16[8,96,192]{2,1,0:T(8,128)(2,1)S(1)}, u32[]{:S(2)}, u32[]{:S(2)}) async-start(bf16[8,96,192]{2,1,0:T(8,128)(2,1)} %shard_map.48), calls=%async_computation | async-start | bytes 786432 | tf_op jit(solution)/shard_map/all_to_all | solution.py:189
  64.7 0.0 collective-permute-done.1
  64.8 0.0 copy-done.4
  64.8 0.0 copy-start
  64.8 2.3 %copy-done = bf16[4,96,6144]{2,1,0:T(8,128)(2,1)S(1)} copy-done((bf16[4,96,6144]{2,1,0:T(8,128)(2,1)S(1)}, bf16[4,96,6144]{2,1,0:T(8,128)(2,1)}, u32[]{:S(2)}) %copy-start) | copy-done | bytes 4718616
  67.1 0.0 copy-start.3
  67.1 2.5 %shard_map.47 = bf16[192,384]{1,0:T(8,128)(2,1)S(1)} custom-call(s32[64]{0:T(128)S(1)} %copy-done.4, bf16[2,16,144,128]{3,2,1,0:T(8,128)(2,1)S(1)} %bitcast.6, bf16[2,16,144,128]{3,2,1,0:T(8,128)(2,1)S(1)} %bitcast.7, bf16[4,96,6144]{2,1,0:T(8,128)(2,1)S(1)} %copy-done), custom_call_target="tpu_custom_call" | custom-call | tf_op jit(solution)/shard_map/pallas_call | solution.py:165
  69.6 2.0 %all-gather = bf16[384,384]{1,0:T(8,128)(2,1)S(1)} all-gather(bf16[192,384]{1,0:T(8,128)(2,1)S(1)} %shard_map.47), channel_id=2, replica_groups={{0,8},{16,24},{32,40},{48,56},{64,72},{80,88},{96,104},{112,120},{128,1..., dimensions={0}, use_global_device_ids=true | all-gather | bytes 442368 | tf_op jit(solution)/shard_map/all_gather | solution.py:198
  71.7 3.6 %all-to-all-done.rows_ref = bf16[8,96,192]{2,1,0:T(8,128)(2,1)S(1)} async-done(((bf16[8,96,192]{2,1,0:T(8,128)(2,1)}), bf16[8,96,192]{2,1,0:T(8,128)(2,1)S(1)}, u32[]{:S(2)}, u32[]{:S(2)}) %all-to-all-start) | async-done | bytes 294944 | tf_op jit(solution)/shard_map/all_to_all | solution.py:189
  75.2 0.0 copy-done.3
  75.2 1.4 %shard_map.49 = (f32[8,72,128]{2,1,0:T(8,128)S(1)}, bf16[8,72,128]{2,1,0:T(8,128)(2,1)S(1)}) custom-call(bf16[2,192,384]{2,1,0:T(8,128)(2,1)S(1)} %bitcast.8, bf16[8,96,192]{2,1,0:T(8,128)(2,1)S(1)} %all-to-all-done.rows_ref, bf16[192,48]{1,0:T(8,128)(2,1)S(1)} %copy-done.3), custom_call_target="tpu_custom_call" | custom-call | tf_op jit(solution)/shard_map/pallas_call | solution.py:165
  76.7 2.5 %collective-permute-start.2 = (bf16[8,72,128]{2,1,0:T(8,128)(2,1)S(1)}, bf16[8,72,128]{2,1,0:T(8,128)(2,1)S(1)}, u32[]{:S(2)}, u32[]{:S(2)}) collective-permute-start(bf16[8,72,128]{2,1,0:T(8,128)(2,1)S(1)} %get-tuple-element.12), channel_id=1, source_target_pairs={{0,16},{8,24},{16,0},{24,8},{32,48},{40,56},{48,32},{56,40},{64,80... | collective-permute-start | bytes 442376 | tf_op jit(solution)/shard_map/ppermute | solution.py:203
  79.2 4.5 %collective-permute-done.2.other_ref = bf16[8,72,128]{2,1,0:T(8,128)(2,1)S(1)} collective-permute-done((bf16[8,72,128]{2,1,0:T(8,128)(2,1)S(1)}, bf16[8,72,128]{2,1,0:T(8,128)(2,1)S(1)}, u32[]{:S(2)}, u32[]{:S(2)}) %collective-permute-start.2) | collective-permute-done | bytes 147488 | tf_op jit(solution)/shard_map/ppermute | solution.py:203
  83.7 25.0 %all_to_all.10.terms_ref = bf16[16,72,128]{2,1,0:T(8,128)(2,1)S(1)} all-to-all(bf16[16,72,128]{2,1,0:T(8,128)(2,1)S(1)} %shard_map.50), channel_id=1, replica_groups={{0,32,64,96,128,160,192,224,256,288,320,352,384,416,448,480},{8,40,72,1..., dimensions={0} | all-to-all | bytes 589824 | tf_op jit(solution)/shard_map/all_to_all | solution.py:204
  108.7 0.8 shard_map.51
  (2 shorter events, 0.1 us)
Async XLA Ops:
  0.0 0.8 copy-start.1
  40.0 13.9 %copy-start.2 = (bf16[4,96,48]{1,2,0:T(8,128)(2,1)S(1)}, bf16[4,96,48]{1,2,0:T(8,128)(2,1)}, u32[]{:S(2)}) copy-start(bf16[4,96,48]{1,2,0:T(8,128)(2,1)} %param.5) | copy-start | bytes 110596
  40.0 11.9 %collective-permute-start = (bf16[2304,128]{1,0:T(8,128)(2,1)S(1)}, bf16[2304,128]{1,0:T(8,128)(2,1)S(1)}, u32[]{:S(2)}, u32[]{:S(2)}) collective-permute-start(bf16[2304,128]{1,0:T(8,128)(2,1)S(1)} %all_gather.16), channel_id=1, source_target_pairs={{0,16},{8,24},{16,0},{24,8},{32,48},{40,56},{48,32},{56,40},{64,80... | collective-permute-start | bytes 1769480 | tf_op jit(solution)/shard_map/ppermute | solution.py:185
  43.6 21.1 %copy-start.4 = (s32[64]{0:T(128)S(1)}, s32[64]{0:T(128)}, u32[]{:S(2)}) copy-start(s32[64]{0:T(128)} %live_ref.1) | copy-start | bytes 772
  52.0 12.7 %collective-permute-start.1 = (bf16[4608,128]{1,0:T(8,128)(2,1)S(1)}, bf16[4608,128]{1,0:T(8,128)(2,1)S(1)}, u32[]{:S(2)}, u32[]{:S(2)}) collective-permute-start(bf16[4608,128]{1,0:T(8,128)(2,1)S(1)} %constant_dynamic-update-slice_fusion), channel_id=1, source_target_pairs={{0,8},{8,0},{16,24},{24,16},{32,40},{40,32},{48,56},{56,48},{64,72... | collective-permute-start | bytes 3538952 | tf_op jit(solution)/shard_map/ppermute | solution.py:191
  57.8 17.4 %all-to-all-start = ((bf16[8,96,192]{2,1,0:T(8,128)(2,1)}), bf16[8,96,192]{2,1,0:T(8,128)(2,1)S(1)}, u32[]{:S(2)}, u32[]{:S(2)}) async-start(bf16[8,96,192]{2,1,0:T(8,128)(2,1)} %shard_map.48), calls=%async_computation | async-start | bytes 786432 | tf_op jit(solution)/shard_map/all_to_all | solution.py:189
  64.8 2.3 %copy-start = (bf16[4,96,6144]{2,1,0:T(8,128)(2,1)S(1)}, bf16[4,96,6144]{2,1,0:T(8,128)(2,1)}, u32[]{:S(2)}) copy-start(bf16[4,96,6144]{2,1,0:T(8,128)(2,1)} %integrals_ref.1) | copy-start | bytes 14155780
  67.1 8.1 %copy-start.3 = (bf16[192,48]{1,0:T(8,128)(2,1)S(1)}, bf16[192,48]{1,0:T(8,128)(2,1)}, u32[]{:S(2)}) copy-start(bf16[192,48]{1,0:T(8,128)(2,1)} %constant.2.clone.signs_ref) | copy-start | bytes 55300
  76.7 7.0 %collective-permute-start.2 = (bf16[8,72,128]{2,1,0:T(8,128)(2,1)S(1)}, bf16[8,72,128]{2,1,0:T(8,128)(2,1)S(1)}, u32[]{:S(2)}, u32[]{:S(2)}) collective-permute-start(bf16[8,72,128]{2,1,0:T(8,128)(2,1)S(1)} %get-tuple-element.12), channel_id=1, source_target_pairs={{0,16},{8,24},{16,0},{24,8},{32,48},{40,56},{48,32},{56,40},{64,80... | collective-permute-start | bytes 442376 | tf_op jit(solution)/shard_map/ppermute | solution.py:203

commit v3 on v2

v3 whole, which is shorter than its diff:
```python
import jax
import jax.numpy as jnp
import numpy as np
from jax import lax
from jax.experimental import pallas as pl
from jax.experimental.pallas import tpu as pltpu
from jax.sharding import PartitionSpec as P

S, K, PQ, PLANES, Q, SPIN = 96, 48, 4, 16, 4, 8
J = K // Q
PLANE = Q * S
CK = 4 * K
PACKED = CK * S // 128

FOLD = [0, 1, 3, 2]
NEAR = [[4 * (4 * h + l) + q for l in FOLD] for h in range(4) for q in range(Q)]
FAR = [[4 * (4 * h + l) + q for h in range(4)] for l in range(4) for q in range(Q)]
LINE = [[4 * z + q for z in range(PLANES)] for q in range(Q)]
CHIP = [[2 * i, 2 * i + 1] for i in range(Q * PLANES // 2)]
ACROSS = [[4 * z + c, 4 * z + 2 + c] for z in range(PLANES) for c in range(2)]
ROWS = [[SPIN * (2 * i + c) + 2 * y + x for c in range(2) for y in range(4)] for i in range(Q * PLANES // 2) for x in range(2)]


def swap(bit, size=Q * PLANES):
    return [(i, i ^ bit) for i in range(size)]


def signs():
    table = (
        ((0, 1), (1, 1), (2, 1), (3, 1)),
        ((1, 1), (0, -1), (3, 1), (2, -1)),
        ((2, -1), (3, 1), (0, 1), (1, -1)),
        ((3, 1), (2, 1), (1, -1), (0, -1)),
    )
    out = np.zeros((4, 4, J, 4, J), np.float32)
    for v, row in enumerate(table):
        for c, (source, sign) in enumerate(row):
            for j in range(J):
                out[c, v, j, source, j] = sign
    return out.reshape(CK, 4 * J)


def nt(a, b):
    return lax.dot_general(a, b, (((1,), (1,)), ((), ())), preferred_element_type=jnp.float32)


def turn(x, lanes):
    return x if lanes == 0 else jnp.concatenate([x[:, 128 - lanes :], x[:, : 128 - lanes]], axis=1)


def pack_kernel(coef_ref, out_ref, rows_ref):
    q = lax.axis_index("pair") % Q
    full = coef_ref[...].reshape(CK, S)
    tail = full[PACKED:]
    side = jnp.concatenate([tail[:, 32 * i : 32 * i + 32] for i in range(3)], axis=0)
    packed = jnp.concatenate([full[:PACKED], side], axis=1)
    turned = packed
    for place in range(1, Q):
        turned = jnp.where(q == place, turn(packed, S * place % 128), turned)
    out_ref[...] = turned
    row = lax.broadcasted_iota(jnp.int32, (CK, CK), 0)
    core = (row >= 8 * J).astype(jnp.int32)
    row = row - 8 * J * core
    x = (row >= 4 * J).astype(jnp.int32)
    row = row - 4 * J * x
    component = sum((row >= J * c).astype(jnp.int32) for c in range(1, 4))
    wanted = (K - J) * component + row + J * (2 * x + core)
    pick = (lax.broadcasted_iota(jnp.int32, (CK, CK), 1) == wanted).astype(jnp.bfloat16)
    rows_ref[...] = jnp.dot(pick, full, preferred_element_type=jnp.float32).astype(jnp.bfloat16)


def plane_of(blocks, lane):
    p0, p1, p2, p3 = blocks
    main = [jnp.where(lane < 96, p0, p1), jnp.where(lane < 64, p1, p2), jnp.where(lane < 32, p2, p3)]
    side = jnp.where(lane < 32, p3, jnp.where(lane < 64, p2, jnp.where(lane < 96, p1, p0)))
    turned = [turn(side[K * i : K * i + K], 32 * (i + 1)) for i in range(3)]
    low = lane[:K]
    tail = [
        jnp.where((low >= 32) & (low < 64), turned[(t + 1) % 3], jnp.where((low >= 64) & (low < 96), turned[(t + 2) % 3], turned[t]))
        for t in range(3)
    ]
    return jnp.concatenate([jnp.concatenate(main, axis=1), jnp.concatenate(tail, axis=1)], axis=0)


def half_kernel(live_ref, own_ref, other_ref, integrals_ref, half_ref, part_ref, arrived):
    copies = []
    for h in range(4):
        columns = integrals_ref.at[:, :, pl.ds(h * 4 * PLANE, 4 * PLANE)]
        copies.append(pltpu.make_async_copy(columns, part_ref.at[h], arrived.at[h]))
        copies[h].start()
    here = lax.axis_index("pair")
    x, core = here % Q // 2, here % 2
    lane = lax.broadcasted_iota(jnp.int32, (PACKED, 128), 1)
    total = None
    for h in range(4):
        planes = []
        for l in range(4):
            slot = FOLD.index(l) * 4 + h
            blocks = []
            for place in range(Q):
                column = (place // 2) ^ x
                blocks.append(jnp.where(core == place % 2, own_ref[column, slot], other_ref[column, slot]))
            planes.append(plane_of(blocks, lane))
        copies[h].wait()
        term = nt(jnp.concatenate(planes, axis=1), part_ref[h].reshape(PQ * S, 4 * PLANE))
        total = term if total is None else total + term
    keep = lax.broadcasted_iota(jnp.int32, (CK, S), 1) < live_ref[here]
    for pq in range(PQ):
        part = jnp.where(keep, total[:, pq * S : (pq + 1) * S], 0.0)
        row = jnp.concatenate([part[c * K : (c + 1) * K] for c in range(4)], axis=1)
        half_ref[pq * K : (pq + 1) * K, :] = row.astype(jnp.bfloat16)


def rows_kernel(own_ref, other_ref, out_ref):
    for place, ref in enumerate((own_ref, other_ref)):
        for core in range(2):
            rows = ref[8 * J * core : 8 * J * (core + 1)]
            for y in range(4):
                out_ref[4 * core + y, place] = rows


def term_kernel(half_ref, rows_ref, signs_ref, keep_ref, give_ref):
    x = lax.axis_index("pair") % Q // 2
    side = lax.axis_index("spin") % 2
    half = [jnp.concatenate([half_ref[core, :, c * S : (c + 1) * S] for core in range(2)], axis=1) for c in range(4)]
    for column, ref in ((x, keep_ref), (x ^ 1, give_ref)):
        signed = []
        for e in range(SPIN):
            rows = jnp.concatenate([rows_ref[4 * core + e // 2, (e % 2) ^ side, column] for core in range(2)], axis=1)
            signed.append(jnp.dot(signs_ref[...], rows, preferred_element_type=jnp.float32).astype(jnp.bfloat16))
        term = None
        for c in range(4):
            more = nt(jnp.concatenate([part[4 * J * c : 4 * J * (c + 1)] for part in signed], axis=0), half[c])
            term = more if term is None else term + more
        for e in range(SPIN):
            part = term[e * 4 * J : (e + 1) * 4 * J]
            tail = jnp.concatenate([part[: 2 * J, 128:], part[2 * J :, 128:]], axis=1)
            ref[e] = jnp.concatenate([part[:, :128], tail], axis=0).astype(ref.dtype)


def join_kernel(keep_ref, given_ref, out_ref):
    partner = 1 - lax.axis_index("pair") % Q // 2
    for e in range(SPIN):
        block = (keep_ref[e] + given_ref[partner, e].astype(jnp.float32)).astype(jnp.bfloat16)
        out_ref[2 * e] = block
        out_ref[2 * e + 1] = block


def sum_kernel(terms_ref, out_ref):
    total = terms_ref[0].astype(jnp.float32)
    for z in range(1, PLANES):
        total = total + terms_ref[z].astype(jnp.float32)
    side = total[4 * J :]
    full = jnp.concatenate([total[: 4 * J], jnp.concatenate([side[:, :64], side[:, 64:]], axis=0)], axis=1)
    real, imag, real_bar, imag_bar = (full[v * J : (v + 1) * J] for v in range(4))
    barred = (lax.axis_index("pair") // Q) % 2 == 1
    parts = (
        (jnp.where(barred, real_bar, real), jnp.where(barred, real, -real_bar)),
        (jnp.where(barred, imag_bar, imag), jnp.where(barred, -imag, imag_bar)),
    )
    for t, (unbarred, partner) in enumerate(parts):
        for pq in range(PQ):
            columns = slice(pq * K, (pq + 1) * K)
            out_ref[t, :, pq, :] = jnp.concatenate([unbarred[:, columns], partner[:, columns]], axis=1)


def call(kernel, out_shape, in_specs=None, mib=16, **more):
    vmem = pl.BlockSpec(memory_space=pltpu.VMEM)

    def run(*args):
        return pl.pallas_call(
            kernel,
            out_shape=out_shape,
            in_specs=in_specs or [vmem] * len(args),
            out_specs=jax.tree.map(lambda _: vmem, out_shape),
            compiler_params=pltpu.CompilerParams(vmem_limit_bytes=mib * 1024 * 1024),
            **more,
        )(*args)

    return run


def shards(integrals, coef, live):
    bf16 = jnp.bfloat16
    shape = jax.ShapeDtypeStruct
    vmem = pl.BlockSpec(memory_space=pltpu.VMEM)
    coef = coef.transpose(0, 2, 1)
    packed, rows = call(pack_kernel, (shape((PACKED, 128), bf16), shape((CK, S), bf16)))(coef)
    line = lax.all_gather(packed, "pair", axis_index_groups=FAR, tiled=True)
    line = lax.all_gather(line, "pair", axis_index_groups=NEAR, tiled=True)
    line, rows = lax.optimization_barrier((line, rows))
    column = lax.ppermute(line, "pair", swap(2))
    rows = call(rows_kernel, shape((8, 2, 8 * J, S), bf16))(rows, lax.ppermute(rows, "spin", swap(1, SPIN)))
    column, rows = lax.optimization_barrier((column, rows))
    rows = lax.all_to_all(rows, ("pair", "spin"), 0, 0, axis_index_groups=ROWS).reshape(8, 2, 2, 4 * J, S)

    own = jnp.concatenate([line, column])
    other = lax.ppermute(own, "pair", swap(1))
    half = call(
        half_kernel,
        shape((PQ * K, 4 * S), bf16),
        [pl.BlockSpec(memory_space=pltpu.SMEM), vmem, vmem, pl.BlockSpec(memory_space=pltpu.HBM)],
        50,
        scratch_shapes=[pltpu.VMEM((4, PQ, S, 4 * PLANE), bf16), pltpu.SemaphoreType.DMA((4,))],
    )(live, own.reshape(2, PLANES, PACKED, 128), other.reshape(2, PLANES, PACKED, 128), integrals)
    halves = lax.all_gather(half, "pair", axis_index_groups=CHIP)
    sign = jnp.asarray(signs(), bf16)
    keep, give = call(term_kernel, (shape((SPIN, 72, 128), jnp.float32), shape((SPIN, 72, 128), bf16)))(halves, rows, sign)
    given = lax.all_gather(give, "pair", axis_index_groups=ACROSS)
    terms = call(join_kernel, shape((PLANES, 72, 128), bf16))(keep, given)
    terms = lax.all_to_all(terms, "pair", 0, 0, axis_index_groups=LINE)
    out = call(sum_kernel, shape((2, J, PQ, 2 * K), jnp.float32))(terms)
    return out.transpose(0, 2, 3, 1)


def solution(mesh):
    placed = (P(None, "pair", None), P(None, "pair", "spin"), P())
    return jax.shard_map(
        shards, mesh=mesh, in_specs=placed, out_specs=P(None, None, "spin", "pair"), check_vma=False
    )
```

time: 110 us -> 106 us (0.964)
  the two profiles are of different devices: /device:TPU:32 before, /device:TPU:64 now
where the time goes in v3:
time: 106 us
  blocking collectives  74.2 us (70%)
  starting transfers between devices  14.5 us (14%)
  waiting for transfers between devices  8.18 us (8%)
  Pallas kernels  7.75 us (7%)
    all_to_all x1, blocking collectives, shards(): terms = lax.all_to_all(terms, 'pair', 0, 0, axis_index_groups=LINE)  27.4 us
    all_gather x1, blocking collectives, shards(): line = lax.all_gather(packed, 'pair', axis_index_groups=FAR, tiled=True)  24.1 us
    all_gather x1, blocking collectives, shards(): line = lax.all_gather(line, 'pair', axis_index_groups=NEAR, tiled=True)  14 us
    pallas_call x6, Pallas kernels, run(): pl.pallas_call(kernel, out_shape=out_shape, in_specs=in_specs or [vmem] *...  7.75 us
    all_gather x1, blocking collectives, shards(): given = lax.all_gather(give, 'pair', axis_index_groups=ACROSS)  6.58 us
    ppermute x1, waiting for transfers between devices, shards(): lax.ppermute(rows, 'spin', swap(1, SPIN))  6.42 us
    ppermute x1, starting transfers between devices, shards(): lax.ppermute(rows, 'spin', swap(1, SPIN))  4.64 us
    all_to_all x1, starting transfers between devices, shards(): lax.all_to_all(rows, ('pair', 'spin'), 0, 0, axis_index_groups=ROWS)  4.59 us
  transfers between devices with their start and end apart: 4, of which 2 were waited for; matrix products, arithmetic and copies ran while one was open for 0% of the time, Pallas kernels for 5%

profile of v3, /device:TPU:64, one launch (start us, length us, event | category | flops | bytes accessed | tf_op | source)
XLA Modules:
  0.0 105.7 jit_solution(11654125720095541458)
XLA Ops:
  0.0 0.0 copy-start.1
  0.0 0.8 copy-done.1
  0.8 0.2 shard_map.46
  1.0 24.1 %all_gather.18 = bf16[576,128]{1,0:T(8,128)(2,1)S(1)} all-gather(bf16[144,128]{1,0:T(8,128)(2,1)S(1)} %get-tuple-element.13), channel_id=1, replica_groups={{0,128,256,384},{8,136,264,392},{16,144,272,400},{24,152,280,408},{32,1..., dimensions={0}, use_global_device_ids=true | all-gather | bytes 184320 | tf_op jit(solution)/shard_map/all_gather | solution.py:189
  25.1 14.0 %all_gather.19 = bf16[2304,128]{1,0:T(8,128)(2,1)S(1)} all-gather(bf16[576,128]{1,0:T(8,128)(2,1)S(1)} %all_gather.18), channel_id=1, replica_groups={{0,32,96,64},{8,40,104,72},{16,48,112,80},{24,56,120,88},{128,160,224,1..., dimensions={0}, use_global_device_ids=true | all-gather | bytes 737280 | tf_op jit(solution)/shard_map/all_gather | solution.py:190
  39.1 3.4 %collective-permute-start = (bf16[2304,128]{1,0:T(8,128)(2,1)S(1)}, bf16[2304,128]{1,0:T(8,128)(2,1)S(1)}, u32[]{:S(2)}, u32[]{:S(2)}) collective-permute-start(bf16[2304,128]{1,0:T(8,128)(2,1)S(1)} %all_gather.19), channel_id=1, source_target_pairs={{0,16},{8,24},{16,0},{24,8},{32,48},{40,56},{48,32},{56,40},{64,80... | collective-permute-start | bytes 1769480 | tf_op jit(solution)/shard_map/ppermute | solution.py:192
  42.5 4.6 %collective-permute-start.1 = (bf16[192,96]{1,0:T(8,128)(2,1)S(1)}, bf16[192,96]{1,0:T(8,128)(2,1)S(1)}, u32[]{:S(2)}, u32[]{:S(2)}) collective-permute-start(bf16[192,96]{1,0:T(8,128)(2,1)S(1)} %get-tuple-element.16.own_ref), channel_id=1, source_target_pairs={{0,1},{1,0},{2,3},{3,2},{4,5},{5,4},{6,7},{7,6},{8,9},{9,8},{10,11... | collective-permute-start | bytes 110600 | tf_op jit(solution)/shard_map/ppermute | solution.py:193
  47.2 0.0 copy-start.2
  47.2 6.4 %collective-permute-done.1.other_ref = bf16[192,96]{1,0:T(8,128)(2,1)S(1)} collective-permute-done((bf16[192,96]{1,0:T(8,128)(2,1)S(1)}, bf16[192,96]{1,0:T(8,128)(2,1)S(1)}, u32[]{:S(2)}, u32[]{:S(2)}) %collective-permute-start.1) | collective-permute-done | bytes 36896 | tf_op jit(solution)/shard_map/ppermute | solution.py:193
  53.6 0.8 shard_map.47
  54.4 0.0 collective-permute-done
  54.4 0.1 constant_dynamic-update-slice_fusion
  54.5 1.9 %collective-permute-start.2 = (bf16[4608,128]{1,0:T(8,128)(2,1)S(1)}, bf16[4608,128]{1,0:T(8,128)(2,1)S(1)}, u32[]{:S(2)}, u32[]{:S(2)}) collective-permute-start(bf16[4608,128]{1,0:T(8,128)(2,1)S(1)} %constant_dynamic-update-slice_fusion), channel_id=1, source_target_pairs={{0,8},{8,0},{16,24},{24,16},{32,40},{40,32},{48,56},{56,48},{64,72... | collective-permute-start | bytes 3538952 | tf_op jit(solution)/shard_map/ppermute | solution.py:198
  56.4 4.6 %all-to-all-start = ((bf16[8,2,96,96]{3,2,1,0:T(8,128)(2,1)}), bf16[8,2,96,96]{3,2,1,0:T(8,128)(2,1)S(1)}, u32[]{:S(2)}, u32[]{:S(2)}) async-start(bf16[8,2,96,96]{3,2,1,0:T(8,128)(2,1)} %shard_map.47), calls=%async_computation | async-start | bytes 786432 | tf_op jit(solution)/shard_map/all_to_all | solution.py:195
  61.0 0.0 collective-permute-done.2
  61.0 0.0 copy-done.2
  61.0 0.0 copy-start
  61.0 4.4 %shard_map.48 = bf16[192,384]{1,0:T(8,128)(2,1)S(1)} custom-call(s32[64]{0:T(128)S(1)} %copy-done.2, bf16[2,16,144,128]{3,2,1,0:T(8,128)(2,1)S(1)} %bitcast.7, bf16[2,16,144,128]{3,2,1,0:T(8,128)(2,1)S(1)} %bitcast.9, bf16[4,96,6144]{2,1,0:T(8,128)(2,1)} %integrals_ref.1), custom_call_target="tpu_custom_call" | custom-call | tf_op jit(solution)/shard_map/pallas_call | solution.py:171
  65.4 2.2 %all-gather = bf16[384,384]{1,0:T(8,128)(2,1)S(1)} all-gather(bf16[192,384]{1,0:T(8,128)(2,1)S(1)} %shard_map.48), channel_id=2, replica_groups={{0,8},{16,24},{32,40},{48,56},{64,72},{80,88},{96,104},{112,120},{128,1..., dimensions={0}, use_global_device_ids=true | all-gather | bytes 442368 | tf_op jit(solution)/shard_map/all_gather | solution.py:206
  67.6 1.8 %all-to-all-done = bf16[8,2,96,96]{3,2,1,0:T(8,128)(2,1)S(1)} async-done(((bf16[8,2,96,96]{3,2,1,0:T(8,128)(2,1)}), bf16[8,2,96,96]{3,2,1,0:T(8,128)(2,1)S(1)}, u32[]{:S(2)}, u32[]{:S(2)}) %all-to-all-start) | async-done | bytes 294944 | tf_op jit(solution)/shard_map/all_to_all | solution.py:195
  69.3 0.0 copy-done
  69.3 1.5 %shard_map.49 = (f32[8,72,128]{2,1,0:T(8,128)S(1)}, bf16[8,72,128]{2,1,0:T(8,128)(2,1)S(1)}) custom-call(bf16[2,192,384]{2,1,0:T(8,128)(2,1)S(1)} %bitcast.11, bf16[8,2,2,48,96]{4,3,2,1,0:T(8,128)(2,1)S(1)} %bitcast.8, bf16[192,48]{1,0:T(8,128)(2,1)S(1)} %copy-done), custom_call_target="tpu_custom_call" | custom-call | tf_op jit(solution)/shard_map/pallas_call | solution.py:171
  70.8 6.6 %all-gather.1 = bf16[16,72,128]{2,1,0:T(8,128)(2,1)S(1)} all-gather(bf16[8,72,128]{2,1,0:T(8,128)(2,1)S(1)} %get-tuple-element.20), channel_id=3, replica_groups={{0,16},{8,24},{32,48},{40,56},{64,80},{72,88},{96,112},{104,120},{128,1..., dimensions={0}, use_global_device_ids=true | all-gather | bytes 442368 | tf_op jit(solution)/shard_map/all_gather | solution.py:209
  77.5 27.4 %all_to_all.10.terms_ref = bf16[16,72,128]{2,1,0:T(8,128)(2,1)S(1)} all-to-all(bf16[16,72,128]{2,1,0:T(8,128)(2,1)S(1)} %shard_map.50), channel_id=1, replica_groups={{0,32,64,96,128,160,192,224,256,288,320,352,384,416,448,480},{8,40,72,1..., dimensions={0} | all-to-all | bytes 589824 | tf_op jit(solution)/shard_map/all_to_all | solution.py:211
  104.9 0.8 shard_map.51
  (2 shorter events, 0.1 us)
Async XLA Ops:
  0.0 0.8 copy-start.1
  39.1 15.3 %collective-permute-start = (bf16[2304,128]{1,0:T(8,128)(2,1)S(1)}, bf16[2304,128]{1,0:T(8,128)(2,1)S(1)}, u32[]{:S(2)}, u32[]{:S(2)}) collective-permute-start(bf16[2304,128]{1,0:T(8,128)(2,1)S(1)} %all_gather.19), channel_id=1, source_target_pairs={{0,16},{8,24},{16,0},{24,8},{32,48},{40,56},{48,32},{56,40},{64,80... | collective-permute-start | bytes 1769480 | tf_op jit(solution)/shard_map/ppermute | solution.py:192
  42.5 11.1 %collective-permute-start.1 = (bf16[192,96]{1,0:T(8,128)(2,1)S(1)}, bf16[192,96]{1,0:T(8,128)(2,1)S(1)}, u32[]{:S(2)}, u32[]{:S(2)}) collective-permute-start(bf16[192,96]{1,0:T(8,128)(2,1)S(1)} %get-tuple-element.16.own_ref), channel_id=1, source_target_pairs={{0,1},{1,0},{2,3},{3,2},{4,5},{5,4},{6,7},{7,6},{8,9},{9,8},{10,11... | collective-permute-start | bytes 110600 | tf_op jit(solution)/shard_map/ppermute | solution.py:193
  47.2 13.8 %copy-start.2 = (s32[64]{0:T(128)S(1)}, s32[64]{0:T(128)}, u32[]{:S(2)}) copy-start(s32[64]{0:T(128)} %live_ref.1) | copy-start | bytes 772
  54.5 6.5 %collective-permute-start.2 = (bf16[4608,128]{1,0:T(8,128)(2,1)S(1)}, bf16[4608,128]{1,0:T(8,128)(2,1)S(1)}, u32[]{:S(2)}, u32[]{:S(2)}) collective-permute-start(bf16[4608,128]{1,0:T(8,128)(2,1)S(1)} %constant_dynamic-update-slice_fusion), channel_id=1, source_target_pairs={{0,8},{8,0},{16,24},{24,16},{32,40},{40,32},{48,56},{56,48},{64,72... | collective-permute-start | bytes 3538952 | tf_op jit(solution)/shard_map/ppermute | solution.py:198
  56.4 12.9 %all-to-all-start = ((bf16[8,2,96,96]{3,2,1,0:T(8,128)(2,1)}), bf16[8,2,96,96]{3,2,1,0:T(8,128)(2,1)S(1)}, u32[]{:S(2)}, u32[]{:S(2)}) async-start(bf16[8,2,96,96]{3,2,1,0:T(8,128)(2,1)} %shard_map.47), calls=%async_computation | async-start | bytes 786432 | tf_op jit(solution)/shard_map/all_to_all | solution.py:195
  61.0 8.3 %copy-start = (bf16[192,48]{1,0:T(8,128)(2,1)S(1)}, bf16[192,48]{1,0:T(8,128)(2,1)}, u32[]{:S(2)}) copy-start(bf16[192,48]{1,0:T(8,128)(2,1)} %constant.2.clone.signs_ref) | copy-start | bytes 55300

commit v4 on v3

--- a/solution.py
+++ b/solution.py
@@ -66,7 +66,9 @@
     component = sum((row >= J * c).astype(jnp.int32) for c in range(1, 4))
     wanted = (K - J) * component + row + J * (2 * x + core)
     pick = (lax.broadcasted_iota(jnp.int32, (CK, CK), 1) == wanted).astype(jnp.bfloat16)
-    rows_ref[...] = jnp.dot(pick, full, preferred_element_type=jnp.float32).astype(jnp.bfloat16)
+    rows = jnp.dot(pick, full, preferred_element_type=jnp.float32).astype(jnp.bfloat16)
+    for group in range(8):
+        rows_ref[group] = rows[8 * J * (group // 4) : 8 * J * (group // 4 + 1)]
 
 
 def plane_of(blocks, lane):
@@ -111,22 +113,15 @@
         half_ref[pq * K : (pq + 1) * K, :] = row.astype(jnp.bfloat16)
 
 
-def rows_kernel(own_ref, other_ref, out_ref):
-    for place, ref in enumerate((own_ref, other_ref)):
-        for core in range(2):
-            rows = ref[8 * J * core : 8 * J * (core + 1)]
-            for y in range(4):
-                out_ref[4 * core + y, place] = rows
-
-
-def term_kernel(half_ref, rows_ref, signs_ref, keep_ref, give_ref):
+def term_kernel(half_ref, rows_ref, far_rows_ref, signs_ref, keep_ref, give_ref):
     x = lax.axis_index("pair") % Q // 2
     side = lax.axis_index("spin") % 2
     half = [jnp.concatenate([half_ref[core, :, c * S : (c + 1) * S] for core in range(2)], axis=1) for c in range(4)]
     for column, ref in ((x, keep_ref), (x ^ 1, give_ref)):
         signed = []
         for e in range(SPIN):
-            rows = jnp.concatenate([rows_ref[4 * core + e // 2, (e % 2) ^ side, column] for core in range(2)], axis=1)
+            groups = [4 * core + e // 2 for core in range(2)]
+            rows = jnp.concatenate([jnp.where(side == e % 2, rows_ref[g, column], far_rows_ref[g, column]) for g in groups], axis=1)
             signed.append(jnp.dot(signs_ref[...], rows, preferred_element_type=jnp.float32).astype(jnp.bfloat16))
         term = None
         for c in range(4):
@@ -185,14 +180,14 @@
     shape = jax.ShapeDtypeStruct
     vmem = pl.BlockSpec(memory_space=pltpu.VMEM)
     coef = coef.transpose(0, 2, 1)
-    packed, rows = call(pack_kernel, (shape((PACKED, 128), bf16), shape((CK, S), bf16)))(coef)
+    packed, rows = call(pack_kernel, (shape((PACKED, 128), bf16), shape((8, 8 * J, S), bf16)))(coef)
     line = lax.all_gather(packed, "pair", axis_index_groups=FAR, tiled=True)
     line = lax.all_gather(line, "pair", axis_index_groups=NEAR, tiled=True)
     line, rows = lax.optimization_barrier((line, rows))
     column = lax.ppermute(line, "pair", swap(2))
-    rows = call(rows_kernel, shape((8, 2, 8 * J, S), bf16))(rows, lax.ppermute(rows, "spin", swap(1, SPIN)))
+    rows = lax.all_to_all(rows, ("pair", "spin"), 0, 0, axis_index_groups=ROWS)
     column, rows = lax.optimization_barrier((column, rows))
-    rows = lax.all_to_all(rows, ("pair", "spin"), 0, 0, axis_index_groups=ROWS).reshape(8, 2, 2, 4 * J, S)
+    far_rows = lax.ppermute(rows, "spin", swap(1, SPIN))
 
     own = jnp.concatenate([line, column])
     other = lax.ppermute(own, "pair", swap(1))
@@ -205,7 +200,9 @@
     )(live, own.reshape(2, PLANES, PACKED, 128), other.reshape(2, PLANES, PACKED, 128), integrals)
     halves = lax.all_gather(half, "pair", axis_index_groups=CHIP)
     sign = jnp.asarray(signs(), bf16)
-    keep, give = call(term_kernel, (shape((SPIN, 72, 128), jnp.float32), shape((SPIN, 72, 128), bf16)))(halves, rows, sign)
+    keep, give = call(term_kernel, (shape((SPIN, 72, 128), jnp.float32), shape((SPIN, 72, 128), bf16)))(
+        halves, rows.reshape(8, 2, 4 * J, S), far_rows.reshape(8, 2, 4 * J, S), sign
+    )
     given = lax.all_gather(give, "pair", axis_index_groups=ACROSS)
     terms = call(join_kernel, shape((PLANES, 72, 128), bf16))(keep, given)
     terms = lax.all_to_all(terms, "pair", 0, 0, axis_index_groups=LINE)

time: 106 us -> 104 us (0.981)
  waiting for transfers between devices: 8.18 us -> 6.24 us
    ppermute x1, waiting for transfers between devices: 6.42 us -> 0.01 us  [shards(): far_rows = lax.ppermute(rows, 'spin', swap(1, SPIN))]
    all_to_all x1, waiting for transfers between devices: 1.75 us -> 6.23 us  [shards(): rows = lax.all_to_all(rows, ('pair', 'spin'), 0, 0, axis_index_groups=ROWS)]
    pallas_call x6 -> x5, Pallas kernels: 7.75 us -> 7.59 us  [run(): pl.pallas_call(kernel, out_shape=out_shape, in_specs=in_specs or [vmem] *...]
  transfers between devices with their start and end apart: 4 -> 4, of which waited for: 2 -> 1; matrix products, arithmetic and copies ran while one was open for 0% -> 0% of each run, Pallas kernels for 5% -> 4%
where the time goes in v4:
time: 104 us; the launch traced here: 103 us
  blocking collectives  73.9 us (71%)
  starting transfers between devices  14.6 us (14%)
  Pallas kernels  7.59 us (7%)
  waiting for transfers between devices  6.24 us (6%)
    all_to_all x1, blocking collectives, shards(): terms = lax.all_to_all(terms, 'pair', 0, 0, axis_index_groups=LINE)  27.2 us
    all_gather x1, blocking collectives, shards(): line = lax.all_gather(packed, 'pair', axis_index_groups=FAR, tiled=True)  24.1 us
    all_gather x1, blocking collectives, shards(): line = lax.all_gather(line, 'pair', axis_index_groups=NEAR, tiled=True)  14 us
    pallas_call x5, Pallas kernels, run(): pl.pallas_call(kernel, out_shape=out_shape, in_specs=in_specs or [vmem] *...  7.59 us
    all_gather x1, blocking collectives, shards(): given = lax.all_gather(give, 'pair', axis_index_groups=ACROSS)  6.57 us
    all_to_all x1, waiting for transfers between devices, shards(): rows = lax.all_to_all(rows, ('pair', 'spin'), 0, 0, axis_index_groups=ROWS)  6.23 us
    ppermute x1, starting transfers between devices, shards(): far_rows = lax.ppermute(rows, 'spin', swap(1, SPIN))  4.67 us
    all_to_all x1, starting transfers between devices, shards(): rows = lax.all_to_all(rows, ('pair', 'spin'), 0, 0, axis_index_groups=ROWS)  4.48 us
  transfers between devices with their start and end apart: 4, of which 1 were waited for; matrix products, arithmetic and copies ran while one was open for 0% of the time, Pallas kernels for 4%

profile of v4, /device:TPU:64, one launch (start us, length us, event | category | flops | bytes accessed | tf_op | source)
XLA Modules:
  0.0 103.2 jit_solution(4091798417839123221)
XLA Ops:
  0.0 0.0 copy-start.1
  0.0 0.8 copy-done.1
  0.8 0.9 shard_map.46
  1.7 24.1 %all_gather.18 = bf16[576,128]{1,0:T(8,128)(2,1)S(1)} all-gather(bf16[144,128]{1,0:T(8,128)(2,1)S(1)} %get-tuple-element.13), channel_id=1, replica_groups={{0,128,256,384},{8,136,264,392},{16,144,272,400},{24,152,280,408},{32,1..., dimensions={0}, use_global_device_ids=true | all-gather | bytes 184320 | tf_op jit(solution)/shard_map/all_gather | solution.py:184
  25.7 14.0 %all_gather.19 = bf16[2304,128]{1,0:T(8,128)(2,1)S(1)} all-gather(bf16[576,128]{1,0:T(8,128)(2,1)S(1)} %all_gather.18), channel_id=1, replica_groups={{0,32,96,64},{8,40,104,72},{16,48,112,80},{24,56,120,88},{128,160,224,1..., dimensions={0}, use_global_device_ids=true | all-gather | bytes 737280 | tf_op jit(solution)/shard_map/all_gather | solution.py:185
  39.7 3.4 %collective-permute-start = (bf16[2304,128]{1,0:T(8,128)(2,1)S(1)}, bf16[2304,128]{1,0:T(8,128)(2,1)S(1)}, u32[]{:S(2)}, u32[]{:S(2)}) collective-permute-start(bf16[2304,128]{1,0:T(8,128)(2,1)S(1)} %all_gather.19), channel_id=1, source_target_pairs={{0,16},{8,24},{16,0},{24,8},{32,48},{40,56},{48,32},{56,40},{64,80... | collective-permute-start | bytes 1769480 | tf_op jit(solution)/shard_map/ppermute | solution.py:187
  43.1 4.5 %all-to-all-start = ((bf16[8,96,96]{2,1,0:T(8,128)(2,1)}), bf16[8,96,96]{2,1,0:T(8,128)(2,1)S(1)}, u32[]{:S(2)}, u32[]{:S(2)}) async-start(bf16[8,96,96]{2,1,0:T(8,128)(2,1)} %get-tuple-element.16), calls=%async_computation | async-start | bytes 393216 | tf_op jit(solution)/shard_map/all_to_all | solution.py:188
  47.6 0.0 copy-start.2
  47.6 6.2 %all-to-all-done = bf16[8,96,96]{2,1,0:T(8,128)(2,1)S(1)} async-done(((bf16[8,96,96]{2,1,0:T(8,128)(2,1)}), bf16[8,96,96]{2,1,0:T(8,128)(2,1)S(1)}, u32[]{:S(2)}, u32[]{:S(2)}) %all-to-all-start) | async-done | bytes 147488 | tf_op jit(solution)/shard_map/all_to_all | solution.py:188
  53.9 0.0 collective-permute-done
  53.9 0.1 constant_dynamic-update-slice_fusion
  54.0 2.0 %collective-permute-start.1 = (bf16[4608,128]{1,0:T(8,128)(2,1)S(1)}, bf16[4608,128]{1,0:T(8,128)(2,1)S(1)}, u32[]{:S(2)}, u32[]{:S(2)}) collective-permute-start(bf16[4608,128]{1,0:T(8,128)(2,1)S(1)} %constant_dynamic-update-slice_fusion), channel_id=1, source_target_pairs={{0,8},{8,0},{16,24},{24,16},{32,40},{40,32},{48,56},{56,48},{64,72... | collective-permute-start | bytes 3538952 | tf_op jit(solution)/shard_map/ppermute | solution.py:193
  56.0 4.7 %collective-permute-start.2 = (bf16[8,96,96]{2,1,0:T(8,128)(2,1)S(1)}, bf16[8,96,96]{2,1,0:T(8,128)(2,1)S(1)}, u32[]{:S(2)}, u32[]{:S(2)}) collective-permute-start(bf16[8,96,96]{2,1,0:T(8,128)(2,1)S(1)} %all-to-all-done), channel_id=1, source_target_pairs={{0,1},{1,0},{2,3},{3,2},{4,5},{5,4},{6,7},{7,6},{8,9},{9,8},{10,11... | collective-permute-start | bytes 442376 | tf_op jit(solution)/shard_map/ppermute | solution.py:190
  60.7 0.0 collective-permute-done.1
  60.7 0.0 copy-done.2
  60.7 0.0 copy-start
  60.7 4.4 %shard_map.47 = bf16[192,384]{1,0:T(8,128)(2,1)S(1)} custom-call(s32[64]{0:T(128)S(1)} %copy-done.2, bf16[2,16,144,128]{3,2,1,0:T(8,128)(2,1)S(1)} %bitcast.8, bf16[2,16,144,128]{3,2,1,0:T(8,128)(2,1)S(1)} %bitcast.9, bf16[4,96,6144]{2,1,0:T(8,128)(2,1)} %integrals_ref.1), custom_call_target="tpu_custom_call" | custom-call | tf_op jit(solution)/shard_map/pallas_call | solution.py:166
  65.1 2.0 %all-gather = bf16[384,384]{1,0:T(8,128)(2,1)S(1)} all-gather(bf16[192,384]{1,0:T(8,128)(2,1)S(1)} %shard_map.47), channel_id=2, replica_groups={{0,8},{16,24},{32,40},{48,56},{64,72},{80,88},{96,104},{112,120},{128,1..., dimensions={0}, use_global_device_ids=true | all-gather | bytes 442368 | tf_op jit(solution)/shard_map/all_gather | solution.py:201
  67.1 0.0 collective-permute-done.2
  67.1 0.0 copy-done
  67.1 1.5 %shard_map.48 = (f32[8,72,128]{2,1,0:T(8,128)S(1)}, bf16[8,72,128]{2,1,0:T(8,128)(2,1)S(1)}) custom-call(bf16[2,192,384]{2,1,0:T(8,128)(2,1)S(1)} %bitcast.11, bf16[8,2,48,96]{3,2,1,0:T(8,128)(2,1)S(1)} %bitcast.12, bf16[8,2,48,96]{3,2,1,0:T(8,128)(2,1)S(1)} %bitcast.13, bf16[192,48]{1,0:T(8,128)(2,1)S(1)} %copy-done), custom_call_target="tpu_custom_call" | custom-call | tf_op jit(solution)/shard_map/pallas_call | solution.py:166
  68.6 6.6 %all-gather.1 = bf16[16,72,128]{2,1,0:T(8,128)(2,1)S(1)} all-gather(bf16[8,72,128]{2,1,0:T(8,128)(2,1)S(1)} %get-tuple-element.20), channel_id=3, replica_groups={{0,16},{8,24},{32,48},{40,56},{64,80},{72,88},{96,112},{104,120},{128,1..., dimensions={0}, use_global_device_ids=true | all-gather | bytes 442368 | tf_op jit(solution)/shard_map/all_gather | solution.py:206
  75.2 27.2 %all_to_all.10.terms_ref = bf16[16,72,128]{2,1,0:T(8,128)(2,1)S(1)} all-to-all(bf16[16,72,128]{2,1,0:T(8,128)(2,1)S(1)} %shard_map.49), channel_id=1, replica_groups={{0,32,64,96,128,160,192,224,256,288,320,352,384,416,448,480},{8,40,72,1..., dimensions={0} | all-to-all | bytes 589824 | tf_op jit(solution)/shard_map/all_to_all | solution.py:208
  102.4 0.8 shard_map.50
  (2 shorter events, 0.1 us)
Async XLA Ops:
  0.0 0.8 copy-start.1
  39.7 14.2 %collective-permute-start = (bf16[2304,128]{1,0:T(8,128)(2,1)S(1)}, bf16[2304,128]{1,0:T(8,128)(2,1)S(1)}, u32[]{:S(2)}, u32[]{:S(2)}) collective-permute-start(bf16[2304,128]{1,0:T(8,128)(2,1)S(1)} %all_gather.19), channel_id=1, source_target_pairs={{0,16},{8,24},{16,0},{24,8},{32,48},{40,56},{48,32},{56,40},{64,80... | collective-permute-start | bytes 1769480 | tf_op jit(solution)/shard_map/ppermute | solution.py:187
  43.1 10.8 %all-to-all-start = ((bf16[8,96,96]{2,1,0:T(8,128)(2,1)}), bf16[8,96,96]{2,1,0:T(8,128)(2,1)S(1)}, u32[]{:S(2)}, u32[]{:S(2)}) async-start(bf16[8,96,96]{2,1,0:T(8,128)(2,1)} %get-tuple-element.16), calls=%async_computation | async-start | bytes 393216 | tf_op jit(solution)/shard_map/all_to_all | solution.py:188
  47.6 13.1 %copy-start.2 = (s32[64]{0:T(128)S(1)}, s32[64]{0:T(128)}, u32[]{:S(2)}) copy-start(s32[64]{0:T(128)} %live_ref.1) | copy-start | bytes 772
  54.0 6.7 %collective-permute-start.1 = (bf16[4608,128]{1,0:T(8,128)(2,1)S(1)}, bf16[4608,128]{1,0:T(8,128)(2,1)S(1)}, u32[]{:S(2)}, u32[]{:S(2)}) collective-permute-start(bf16[4608,128]{1,0:T(8,128)(2,1)S(1)} %constant_dynamic-update-slice_fusion), channel_id=1, source_target_pairs={{0,8},{8,0},{16,24},{24,16},{32,40},{40,32},{48,56},{56,48},{64,72... | collective-permute-start | bytes 3538952 | tf_op jit(solution)/shard_map/ppermute | solution.py:193
  56.0 11.1 %collective-permute-start.2 = (bf16[8,96,96]{2,1,0:T(8,128)(2,1)S(1)}, bf16[8,96,96]{2,1,0:T(8,128)(2,1)S(1)}, u32[]{:S(2)}, u32[]{:S(2)}) collective-permute-start(bf16[8,96,96]{2,1,0:T(8,128)(2,1)S(1)} %all-to-all-done), channel_id=1, source_target_pairs={{0,1},{1,0},{2,3},{3,2},{4,5},{5,4},{6,7},{7,6},{8,9},{9,8},{10,11... | collective-permute-start | bytes 442376 | tf_op jit(solution)/shard_map/ppermute | solution.py:190
  60.7 6.4 %copy-start = (bf16[192,48]{1,0:T(8,128)(2,1)S(1)}, bf16[192,48]{1,0:T(8,128)(2,1)}, u32[]{:S(2)}) copy-start(bf16[192,48]{1,0:T(8,128)(2,1)} %constant.2.clone.signs_ref) | copy-start | bytes 55300

commit v5 on v4

--- a/solution.py
+++ b/solution.py
@@ -17,6 +17,7 @@
 FAR = [[4 * (4 * h + l) + q for h in range(4)] for l in range(4) for q in range(Q)]
 LINE = [[4 * z + q for z in range(PLANES)] for q in range(Q)]
 CHIP = [[2 * i, 2 * i + 1] for i in range(Q * PLANES // 2)]
+PLANE_PAIRS = [[8 * z + q, 8 * z + 4 + q] for z in range(PLANES // 2) for q in range(Q)]
 ACROSS = [[4 * z + c, 4 * z + 2 + c] for z in range(PLANES) for c in range(2)]
 ROWS = [[SPIN * (2 * i + c) + 2 * y + x for c in range(2) for y in range(4)] for i in range(Q * PLANES // 2) for x in range(2)]
 
@@ -37,7 +38,7 @@
         for c, (source, sign) in enumerate(row):
             for j in range(J):
                 out[c, v, j, source, j] = sign
-    return out.reshape(CK, 4 * J)
+    return np.kron(np.eye(2, dtype=np.float32), out.reshape(CK, 4 * J))
 
 
 def nt(a, b):
@@ -66,9 +67,14 @@
     component = sum((row >= J * c).astype(jnp.int32) for c in range(1, 4))
     wanted = (K - J) * component + row + J * (2 * x + core)
     pick = (lax.broadcasted_iota(jnp.int32, (CK, CK), 1) == wanted).astype(jnp.bfloat16)
-    rows = jnp.dot(pick, full, preferred_element_type=jnp.float32).astype(jnp.bfloat16)
-    for group in range(8):
-        rows_ref[group] = rows[8 * J * (group // 4) : 8 * J * (group // 4 + 1)]
+    rows = jnp.dot(pick, full, preferred_element_type=jnp.float32)
+    for core in range(2):
+        first, second = (rows[4 * J * i : 4 * J * (i + 1)] for i in (2 * core, 2 * core + 1))
+        top = jnp.concatenate([first, second[:, :32]], axis=1)
+        low = jnp.concatenate([second[: 2 * J, 32:], second[2 * J :, 32:]], axis=1)
+        block = jnp.concatenate([top, low], axis=0).astype(jnp.bfloat16)
+        for y in range(4):
+            rows_ref[4 * core + y] = block
 
 
 def plane_of(blocks, lane):
@@ -84,49 +90,60 @@
     return jnp.concatenate([jnp.concatenate(main, axis=1), jnp.concatenate(tail, axis=1)], axis=0)
 
 
-def half_kernel(live_ref, own_ref, other_ref, integrals_ref, half_ref, part_ref, arrived):
-    copies = []
-    for h in range(4):
-        columns = integrals_ref.at[:, :, pl.ds(h * 4 * PLANE, 4 * PLANE)]
-        copies.append(pltpu.make_async_copy(columns, part_ref.at[h], arrived.at[h]))
-        copies[h].start()
+def half_kernel(live_ref, own_ref, other_ref, integrals_ref, half_ref, total_ref):
+    step = pl.program_id(0)
     here = lax.axis_index("pair")
     x, core = here % Q // 2, here % 2
     lane = lax.broadcasted_iota(jnp.int32, (PACKED, 128), 1)
-    total = None
-    for h in range(4):
-        planes = []
-        for l in range(4):
-            slot = FOLD.index(l) * 4 + h
-            blocks = []
-            for place in range(Q):
-                column = (place // 2) ^ x
-                blocks.append(jnp.where(core == place % 2, own_ref[column, slot], other_ref[column, slot]))
-            planes.append(plane_of(blocks, lane))
-        copies[h].wait()
-        term = nt(jnp.concatenate(planes, axis=1), part_ref[h].reshape(PQ * S, 4 * PLANE))
-        total = term if total is None else total + term
-    keep = lax.broadcasted_iota(jnp.int32, (CK, S), 1) < live_ref[here]
-    for pq in range(PQ):
-        part = jnp.where(keep, total[:, pq * S : (pq + 1) * S], 0.0)
-        row = jnp.concatenate([part[c * K : (c + 1) * K] for c in range(4)], axis=1)
-        half_ref[pq * K : (pq + 1) * K, :] = row.astype(jnp.bfloat16)
+    planes = []
+    for i in range(PLANES // 2):
+        slot = FOLD.index(i % 4) * 4 + 2 * step + i // 4
+        blocks = []
+        for place in range(Q):
+            column = (place // 2) ^ x
+            blocks.append(jnp.where(core == place % 2, own_ref[column, slot], other_ref[column, slot]))
+        planes.append(plane_of(blocks, lane))
+    term = nt(jnp.concatenate(planes, axis=1), integrals_ref[...].reshape(PQ * S, PLANES * PLANE // 2))
+
+    @pl.when(step == 0)
+    def _():
+        total_ref[...] = term
+
+    @pl.when(step == 1)
+    def _():
+        total = total_ref[...] + term
+        keep = lax.broadcasted_iota(jnp.int32, (CK, S), 1) < live_ref[here]
+        for pq in range(PQ):
+            part = jnp.where(keep, total[:, pq * S : (pq + 1) * S], 0.0)
+            row = jnp.concatenate([part[c * K : (c + 1) * K] for c in range(4)], axis=1)
+            half_ref[pq * K : (pq + 1) * K, :] = row.astype(jnp.bfloat16)
+
+
+def rows_of(block):
+    block = block.astype(jnp.float32)
+    low = jnp.concatenate([block[4 * J :, :64], block[4 * J :, 64:]], axis=0)
+    return jnp.concatenate([block[: 4 * J, :S], jnp.concatenate([block[: 4 * J, S:], low], axis=1)], axis=0)
 
 
 def term_kernel(half_ref, rows_ref, far_rows_ref, signs_ref, keep_ref, give_ref):
     x = lax.axis_index("pair") % Q // 2
     side = lax.axis_index("spin") % 2
     half = [jnp.concatenate([half_ref[core, :, c * S : (c + 1) * S] for core in range(2)], axis=1) for c in range(4)]
-    for column, ref in ((x, keep_ref), (x ^ 1, give_ref)):
-        signed = []
-        for e in range(SPIN):
-            groups = [4 * core + e // 2 for core in range(2)]
-            rows = jnp.concatenate([jnp.where(side == e % 2, rows_ref[g, column], far_rows_ref[g, column]) for g in groups], axis=1)
-            signed.append(jnp.dot(signs_ref[...], rows, preferred_element_type=jnp.float32).astype(jnp.bfloat16))
+    signed = []
+    for e in range(SPIN):
+        groups = [4 * core + e // 2 for core in range(2)]
+        rows = [rows_of(jnp.where(side == e % 2, rows_ref[g], far_rows_ref[g])) for g in groups]
+        rows = jnp.concatenate(rows, axis=1).astype(jnp.bfloat16)
+        signed.append(jnp.dot(signs_ref[...], rows, preferred_element_type=jnp.float32).astype(jnp.bfloat16))
+    terms = []
+    for column in range(2):
         term = None
         for c in range(4):
-            more = nt(jnp.concatenate([part[4 * J * c : 4 * J * (c + 1)] for part in signed], axis=0), half[c])
+            at = 4 * J * (4 * column + c)
+            more = nt(jnp.concatenate([part[at : at + 4 * J] for part in signed], axis=0), half[c])
             term = more if term is None else term + more
+        terms.append(term)
+    for term, ref in ((jnp.where(x == 0, terms[0], terms[1]), keep_ref), (jnp.where(x == 0, terms[1], terms[0]), give_ref)):
         for e in range(SPIN):
             part = term[e * 4 * J : (e + 1) * 4 * J]
             tail = jnp.concatenate([part[: 2 * J, 128:], part[2 * J :, 128:]], axis=1)
@@ -136,15 +153,20 @@
 def join_kernel(keep_ref, given_ref, out_ref):
     partner = 1 - lax.axis_index("pair") % Q // 2
     for e in range(SPIN):
-        block = (keep_ref[e] + given_ref[partner, e].astype(jnp.float32)).astype(jnp.bfloat16)
-        out_ref[2 * e] = block
-        out_ref[2 * e + 1] = block
+        block = keep_ref[e] + given_ref[partner, e].astype(jnp.float32)
+        out_ref[2 * e] = block[:40].astype(jnp.bfloat16)
+        out_ref[2 * e + 1] = block[32:].astype(jnp.bfloat16)
 
 
 def sum_kernel(terms_ref, out_ref):
     total = terms_ref[0].astype(jnp.float32)
     for z in range(1, PLANES):
         total = total + terms_ref[z].astype(jnp.float32)
+    out_ref[...] = total
+
+
+def result_kernel(sums_ref, out_ref):
+    total = jnp.concatenate([sums_ref[0], sums_ref[1, 8:]], axis=0)
     side = total[4 * J :]
     full = jnp.concatenate([total[: 4 * J], jnp.concatenate([side[:, :64], side[:, 64:]], axis=0)], axis=1)
     real, imag, real_bar, imag_bar = (full[v * J : (v + 1) * J] for v in range(4))
@@ -180,7 +202,7 @@
     shape = jax.ShapeDtypeStruct
     vmem = pl.BlockSpec(memory_space=pltpu.VMEM)
     coef = coef.transpose(0, 2, 1)
-    packed, rows = call(pack_kernel, (shape((PACKED, 128), bf16), shape((8, 8 * J, S), bf16)))(coef)
+    packed, rows = call(pack_kernel, (shape((PACKED, 128), bf16), shape((8, 72, 128), bf16)))(coef)
     line = lax.all_gather(packed, "pair", axis_index_groups=FAR, tiled=True)
     line = lax.all_gather(line, "pair", axis_index_groups=NEAR, tiled=True)
     line, rows = lax.optimization_barrier((line, rows))
@@ -194,19 +216,22 @@
     half = call(
         half_kernel,
         shape((PQ * K, 4 * S), bf16),
-        [pl.BlockSpec(memory_space=pltpu.SMEM), vmem, vmem, pl.BlockSpec(memory_space=pltpu.HBM)],
+        [pl.BlockSpec(memory_space=pltpu.SMEM), vmem, vmem, pl.BlockSpec((PQ, S, PLANES * PLANE // 2), lambda i: (0, 0, i))],
         50,
-        scratch_shapes=[pltpu.VMEM((4, PQ, S, 4 * PLANE), bf16), pltpu.SemaphoreType.DMA((4,))],
+        grid=(2,),
+        scratch_shapes=[pltpu.VMEM((CK, PQ * S), jnp.float32)],
     )(live, own.reshape(2, PLANES, PACKED, 128), other.reshape(2, PLANES, PACKED, 128), integrals)
     halves = lax.all_gather(half, "pair", axis_index_groups=CHIP)
     sign = jnp.asarray(signs(), bf16)
     keep, give = call(term_kernel, (shape((SPIN, 72, 128), jnp.float32), shape((SPIN, 72, 128), bf16)))(
-        halves, rows.reshape(8, 2, 4 * J, S), far_rows.reshape(8, 2, 4 * J, S), sign
+        halves, rows, far_rows, sign
     )
     given = lax.all_gather(give, "pair", axis_index_groups=ACROSS)
-    terms = call(join_kernel, shape((PLANES, 72, 128), bf16))(keep, given)
+    terms = call(join_kernel, shape((PLANES, 40, 128), bf16))(keep, given)
     terms = lax.all_to_all(terms, "pair", 0, 0, axis_index_groups=LINE)
-    out = call(sum_kernel, shape((2, J, PQ, 2 * K), jnp.float32))(terms)
+    sums = call(sum_kernel, shape((40, 128), jnp.float32))(terms)
+    sums = lax.all_gather(sums, "pair", axis_index_groups=PLANE_PAIRS)
+    out = call(result_kernel, shape((2, J, PQ, 2 * K), jnp.float32))(sums)
     return out.transpose(0, 2, 3, 1)
 
 

time: 104 us -> 103 us (level)
  the two profiles are of different devices: /device:TPU:64 before, /device:TPU:32 now
where the time goes in v5:
time: 103 us; the launch traced here: 102 us
  blocking collectives  74.1 us (72%)
  starting transfers between devices  14.6 us (14%)
  Pallas kernels  7.15 us (7%)
  waiting for transfers between devices  5.59 us (5%)
    all_gather x1, blocking collectives, shards(): line = lax.all_gather(packed, 'pair', axis_index_groups=FAR, tiled=True)  25 us
    all_to_all x1, blocking collectives, shards(): terms = lax.all_to_all(terms, 'pair', 0, 0, axis_index_groups=LINE)  22.1 us
    all_gather x1, blocking collectives, shards(): line = lax.all_gather(line, 'pair', axis_index_groups=NEAR, tiled=True)  14 us
    pallas_call x6, Pallas kernels, run(): pl.pallas_call(kernel, out_shape=out_shape, in_specs=in_specs or [vmem] *...  7.15 us
    all_gather x1, blocking collectives, shards(): given = lax.all_gather(give, 'pair', axis_index_groups=ACROSS)  6.58 us
    all_to_all x1, waiting for transfers between devices, shards(): rows = lax.all_to_all(rows, ('pair', 'spin'), 0, 0, axis_index_groups=ROWS)  5.59 us
    ppermute x1, starting transfers between devices, shards(): far_rows = lax.ppermute(rows, 'spin', swap(1, SPIN))  4.65 us
    all_to_all x1, starting transfers between devices, shards(): rows = lax.all_to_all(rows, ('pair', 'spin'), 0, 0, axis_index_groups=ROWS)  4.48 us
  transfers between devices with their start and end apart: 4, of which 1 were waited for; matrix products, arithmetic and copies ran while one was open for 0% of the time, Pallas kernels for 4%

profile of v5, /device:TPU:32, one launch (start us, length us, event | category | flops | bytes accessed | tf_op | source)
XLA Modules:
  0.0 102.5 jit_solution(11319677323663695739)
XLA Ops:
  0.0 0.0 copy-start.1
  0.0 0.8 copy-done.1
  0.8 0.9 shard_map.46
  1.7 25.0 %all_gather.24 = bf16[576,128]{1,0:T(8,128)(2,1)S(1)} all-gather(bf16[144,128]{1,0:T(8,128)(2,1)S(1)} %get-tuple-element.13), channel_id=1, replica_groups={{0,128,256,384},{8,136,264,392},{16,144,272,400},{24,152,280,408},{32,1..., dimensions={0}, use_global_device_ids=true | all-gather | bytes 184320 | tf_op jit(solution)/shard_map/all_gather | solution.py:206
  26.7 14.0 %all_gather.25 = bf16[2304,128]{1,0:T(8,128)(2,1)S(1)} all-gather(bf16[576,128]{1,0:T(8,128)(2,1)S(1)} %all_gather.24), channel_id=1, replica_groups={{0,32,96,64},{8,40,104,72},{16,48,112,80},{24,56,120,88},{128,160,224,1..., dimensions={0}, use_global_device_ids=true | all-gather | bytes 737280 | tf_op jit(solution)/shard_map/all_gather | solution.py:207
  40.7 3.4 %collective-permute-start = (bf16[2304,128]{1,0:T(8,128)(2,1)S(1)}, bf16[2304,128]{1,0:T(8,128)(2,1)S(1)}, u32[]{:S(2)}, u32[]{:S(2)}) collective-permute-start(bf16[2304,128]{1,0:T(8,128)(2,1)S(1)} %all_gather.25), channel_id=1, source_target_pairs={{0,16},{8,24},{16,0},{24,8},{32,48},{40,56},{48,32},{56,40},{64,80... | collective-permute-start | bytes 1769480 | tf_op jit(solution)/shard_map/ppermute | solution.py:209
  44.1 4.5 %all-to-all-start = ((bf16[8,72,128]{2,1,0:T(8,128)(2,1)}), bf16[8,72,128]{2,1,0:T(8,128)(2,1)S(1)}, u32[]{:S(2)}, u32[]{:S(2)}) async-start(bf16[8,72,128]{2,1,0:T(8,128)(2,1)} %get-tuple-element.16), calls=%async_computation | async-start | bytes 294912 | tf_op jit(solution)/shard_map/all_to_all | solution.py:210
  48.5 0.0 copy-start.2
  48.6 5.6 %all-to-all-done.rows_ref = bf16[8,72,128]{2,1,0:T(8,128)(2,1)S(1)} async-done(((bf16[8,72,128]{2,1,0:T(8,128)(2,1)}), bf16[8,72,128]{2,1,0:T(8,128)(2,1)S(1)}, u32[]{:S(2)}, u32[]{:S(2)}) %all-to-all-start) | async-done | bytes 147488 | tf_op jit(solution)/shard_map/all_to_all | solution.py:210
  54.2 0.0 collective-permute-done
  54.2 0.1 constant_dynamic-update-slice_fusion
  54.3 2.1 %collective-permute-start.1 = (bf16[4608,128]{1,0:T(8,128)(2,1)S(1)}, bf16[4608,128]{1,0:T(8,128)(2,1)S(1)}, u32[]{:S(2)}, u32[]{:S(2)}) collective-permute-start(bf16[4608,128]{1,0:T(8,128)(2,1)S(1)} %constant_dynamic-update-slice_fusion), channel_id=1, source_target_pairs={{0,8},{8,0},{16,24},{24,16},{32,40},{40,32},{48,56},{56,48},{64,72... | collective-permute-start | bytes 3538952 | tf_op jit(solution)/shard_map/ppermute | solution.py:215
  56.4 4.7 %collective-permute-start.2 = (bf16[8,72,128]{2,1,0:T(8,128)(2,1)S(1)}, bf16[8,72,128]{2,1,0:T(8,128)(2,1)S(1)}, u32[]{:S(2)}, u32[]{:S(2)}) collective-permute-start(bf16[8,72,128]{2,1,0:T(8,128)(2,1)S(1)} %all-to-all-done.rows_ref), channel_id=1, source_target_pairs={{0,1},{1,0},{2,3},{3,2},{4,5},{5,4},{6,7},{7,6},{8,9},{9,8},{10,11... | collective-permute-start | bytes 442376 | tf_op jit(solution)/shard_map/ppermute | solution.py:212
  61.0 0.0 collective-permute-done.1
  61.1 0.0 copy-done.2
  61.1 0.0 copy-start
  61.1 4.0 %shard_map.47 = bf16[192,384]{1,0:T(8,128)(2,1)S(1)} custom-call(s32[64]{0:T(128)S(1)} %copy-done.2, bf16[2,16,144,128]{3,2,1,0:T(8,128)(2,1)S(1)} %bitcast.7, bf16[2,16,144,128]{3,2,1,0:T(8,128)(2,1)S(1)} %bitcast.8, bf16[4,96,6144]{2,1,0:T(8,128)(2,1)} %integrals_ref.1), custom_call_target="tpu_custom_call" | custom-call | tf_op jit(solution)/shard_map/pallas_call | solution.py:188
  65.1 2.0 %all-gather = bf16[384,384]{1,0:T(8,128)(2,1)S(1)} all-gather(bf16[192,384]{1,0:T(8,128)(2,1)S(1)} %shard_map.47), channel_id=2, replica_groups={{0,8},{16,24},{32,40},{48,56},{64,72},{80,88},{96,104},{112,120},{128,1..., dimensions={0}, use_global_device_ids=true | all-gather | bytes 442368 | tf_op jit(solution)/shard_map/all_gather | solution.py:224
  67.1 0.0 collective-permute-done.2.far_rows_ref
  67.1 0.0 copy-done
  67.1 1.4 %shard_map.48 = (f32[8,72,128]{2,1,0:T(8,128)S(1)}, bf16[8,72,128]{2,1,0:T(8,128)(2,1)S(1)}) custom-call(bf16[2,192,384]{2,1,0:T(8,128)(2,1)S(1)} %bitcast.9, bf16[8,72,128]{2,1,0:T(8,128)(2,1)S(1)} %all-to-all-done.rows_ref, bf16[8,72,128]{2,1,0:T(8,128)(2,1)S(1)} %collective-permute-done.2.far_rows_ref, bf16[384,96]{1,0:T(8,128)(2,1)S(1)} %copy-done), custom_call_target="tpu_custom_call" | custom-call | tf_op jit(solution)/shard_map/pallas_call | solution.py:188
  68.5 6.6 %all-gather.1 = bf16[16,72,128]{2,1,0:T(8,128)(2,1)S(1)} all-gather(bf16[8,72,128]{2,1,0:T(8,128)(2,1)S(1)} %get-tuple-element.20), channel_id=3, replica_groups={{0,16},{8,24},{32,48},{40,56},{64,80},{72,88},{96,112},{104,120},{128,1..., dimensions={0}, use_global_device_ids=true | all-gather | bytes 442368 | tf_op jit(solution)/shard_map/all_gather | solution.py:229
  75.1 22.1 %all_to_all.10.terms_ref = bf16[16,40,128]{2,1,0:T(8,128)(2,1)S(1)} all-to-all(bf16[16,40,128]{2,1,0:T(8,128)(2,1)S(1)} %shard_map.49), channel_id=1, replica_groups={{0,32,64,96,128,160,192,224,256,288,320,352,384,416,448,480},{8,40,72,1..., dimensions={0} | all-to-all | bytes 327680 | tf_op jit(solution)/shard_map/all_to_all | solution.py:231
  97.2 4.5 %all-gather.2 = f32[80,128]{1,0:T(8,128)S(1)} all-gather(f32[40,128]{1,0:T(8,128)S(1)} %shard_map.50), channel_id=4, replica_groups={{0,32},{8,40},{16,48},{24,56},{64,96},{72,104},{80,112},{88,120},{128,1..., dimensions={0}, use_global_device_ids=true | all-gather | bytes 61440 | tf_op jit(solution)/shard_map/all_gather | solution.py:233
  101.7 0.8 shard_map.51
  (3 shorter events, 0.1 us)
Async XLA Ops:
  0.0 0.8 copy-start.1
  40.7 13.5 %collective-permute-start = (bf16[2304,128]{1,0:T(8,128)(2,1)S(1)}, bf16[2304,128]{1,0:T(8,128)(2,1)S(1)}, u32[]{:S(2)}, u32[]{:S(2)}) collective-permute-start(bf16[2304,128]{1,0:T(8,128)(2,1)S(1)} %all_gather.25), channel_id=1, source_target_pairs={{0,16},{8,24},{16,0},{24,8},{32,48},{40,56},{48,32},{56,40},{64,80... | collective-permute-start | bytes 1769480 | tf_op jit(solution)/shard_map/ppermute | solution.py:209
  44.1 10.1 %all-to-all-start = ((bf16[8,72,128]{2,1,0:T(8,128)(2,1)}), bf16[8,72,128]{2,1,0:T(8,128)(2,1)S(1)}, u32[]{:S(2)}, u32[]{:S(2)}) async-start(bf16[8,72,128]{2,1,0:T(8,128)(2,1)} %get-tuple-element.16), calls=%async_computation | async-start | bytes 294912 | tf_op jit(solution)/shard_map/all_to_all | solution.py:210
  48.5 12.5 %copy-start.2 = (s32[64]{0:T(128)S(1)}, s32[64]{0:T(128)}, u32[]{:S(2)}) copy-start(s32[64]{0:T(128)} %live_ref.1) | copy-start | bytes 772
  54.3 6.8 %collective-permute-start.1 = (bf16[4608,128]{1,0:T(8,128)(2,1)S(1)}, bf16[4608,128]{1,0:T(8,128)(2,1)S(1)}, u32[]{:S(2)}, u32[]{:S(2)}) collective-permute-start(bf16[4608,128]{1,0:T(8,128)(2,1)S(1)} %constant_dynamic-update-slice_fusion), channel_id=1, source_target_pairs={{0,8},{8,0},{16,24},{24,16},{32,40},{40,32},{48,56},{56,48},{64,72... | collective-permute-start | bytes 3538952 | tf_op jit(solution)/shard_map/ppermute | solution.py:215
  56.4 10.7 %collective-permute-start.2 = (bf16[8,72,128]{2,1,0:T(8,128)(2,1)S(1)}, bf16[8,72,128]{2,1,0:T(8,128)(2,1)S(1)}, u32[]{:S(2)}, u32[]{:S(2)}) collective-permute-start(bf16[8,72,128]{2,1,0:T(8,128)(2,1)S(1)} %all-to-all-done.rows_ref), channel_id=1, source_target_pairs={{0,1},{1,0},{2,3},{3,2},{4,5},{5,4},{6,7},{7,6},{8,9},{9,8},{10,11... | collective-permute-start | bytes 442376 | tf_op jit(solution)/shard_map/ppermute | solution.py:212
  61.1 6.0 %copy-start = (bf16[384,96]{1,0:T(8,128)(2,1)S(1)}, bf16[384,96]{1,0:T(8,128)(2,1)}, u32[]{:S(2)}) copy-start(bf16[384,96]{1,0:T(8,128)(2,1)} %constant.2.clone.signs_ref) | copy-start | bytes 221188

commit v6 on v5

--- a/solution.py
+++ b/solution.py
@@ -208,7 +208,7 @@
     line, rows = lax.optimization_barrier((line, rows))
     column = lax.ppermute(line, "pair", swap(2))
     rows = lax.all_to_all(rows, ("pair", "spin"), 0, 0, axis_index_groups=ROWS)
-    column, rows = lax.optimization_barrier((column, rows))
+    line, column, rows = lax.optimization_barrier((line, column, rows))
     far_rows = lax.ppermute(rows, "spin", swap(1, SPIN))
 
     own = jnp.concatenate([line, column])

time: 103 us -> 102 us (level)
  blocking collectives: 74.1 us -> 84 us
  waiting for transfers between devices: 5.59 us -> 0.01 us
  starting transfers between devices: 14.6 us -> 10.2 us
    all_to_all x0 -> x1, blocking collectives: none -> 9.9 us  [shards(): rows = lax.all_to_all(rows, ('pair', 'spin'), 0, 0, axis_index_groups=ROWS)]
    all_to_all x1 -> x0, waiting for transfers between devices: 5.59 us -> none  [shards(): rows = lax.all_to_all(rows, ('pair', 'spin'), 0, 0, axis_index_groups=ROWS)]
    all_to_all x1 -> x0, starting transfers between devices: 4.48 us -> none  [shards(): rows = lax.all_to_all(rows, ('pair', 'spin'), 0, 0, axis_index_groups=ROWS)]
  transfers between devices with their start and end apart: 4 -> 3, of which waited for: 1 -> 0; matrix products, arithmetic and copies ran while one was open for 0% -> 0% of each run, Pallas kernels for 4% -> 4%
where the time goes in v6:
time: 102 us
  blocking collectives  84 us (82%)
  starting transfers between devices  10.2 us (10%)
  Pallas kernels  6.51 us (6%)
    all_gather x1, blocking collectives, shards(): line = lax.all_gather(packed, 'pair', axis_index_groups=FAR, tiled=True)  25 us
    all_to_all x1, blocking collectives, shards(): terms = lax.all_to_all(terms, 'pair', 0, 0, axis_index_groups=LINE)  22.1 us
    all_gather x1, blocking collectives, shards(): line = lax.all_gather(line, 'pair', axis_index_groups=NEAR, tiled=True)  14 us
    all_to_all x1, blocking collectives, shards(): rows = lax.all_to_all(rows, ('pair', 'spin'), 0, 0, axis_index_groups=ROWS)  9.9 us
    all_gather x1, blocking collectives, shards(): given = lax.all_gather(give, 'pair', axis_index_groups=ACROSS)  6.58 us
    pallas_call x6, Pallas kernels, run(): pl.pallas_call(kernel, out_shape=out_shape, in_specs=in_specs or [vmem] *...  6.51 us
    ppermute x1, starting transfers between devices, shards(): far_rows = lax.ppermute(rows, 'spin', swap(1, SPIN))  4.65 us
    all_gather x1, blocking collectives, shards(): sums = lax.all_gather(sums, 'pair', axis_index_groups=PLANE_PAIRS)  4.46 us
  transfers between devices with their start and end apart: 3, of which 0 were waited for; matrix products, arithmetic and copies ran while one was open for 0% of the time, Pallas kernels for 4%

profile of v6, /device:TPU:32, one launch (start us, length us, event | category | flops | bytes accessed | tf_op | source)
XLA Modules:
  0.0 101.7 jit_solution(18404041734020624773)
XLA Ops:
  0.0 0.0 copy-start.1
  0.0 0.8 copy-done.1
  0.8 0.2 shard_map.46
  1.1 25.0 %all_gather.24 = bf16[576,128]{1,0:T(8,128)(2,1)S(1)} all-gather(bf16[144,128]{1,0:T(8,128)(2,1)S(1)} %get-tuple-element.14), channel_id=1, replica_groups={{0,128,256,384},{8,136,264,392},{16,144,272,400},{24,152,280,408},{32,1..., dimensions={0}, use_global_device_ids=true | all-gather | bytes 184320 | tf_op jit(solution)/shard_map/all_gather | solution.py:206
  26.0 14.0 %all_gather.25 = bf16[2304,128]{1,0:T(8,128)(2,1)S(1)} all-gather(bf16[576,128]{1,0:T(8,128)(2,1)S(1)} %all_gather.24), channel_id=1, replica_groups={{0,32,96,64},{8,40,104,72},{16,48,112,80},{24,56,120,88},{128,160,224,1..., dimensions={0}, use_global_device_ids=true | all-gather | bytes 737280 | tf_op jit(solution)/shard_map/all_gather | solution.py:207
  40.0 3.4 %collective-permute-start = (bf16[2304,128]{1,0:T(8,128)(2,1)S(1)}, bf16[2304,128]{1,0:T(8,128)(2,1)S(1)}, u32[]{:S(2)}, u32[]{:S(2)}) collective-permute-start(bf16[2304,128]{1,0:T(8,128)(2,1)S(1)} %all_gather.25), channel_id=1, source_target_pairs={{0,16},{8,24},{16,0},{24,8},{32,48},{40,56},{48,32},{56,40},{64,80... | collective-permute-start | bytes 1769480 | tf_op jit(solution)/shard_map/ppermute | solution.py:209
  43.4 9.9 %all_to_all.10.rows_ref = bf16[8,72,128]{2,1,0:T(8,128)(2,1)S(1)} all-to-all(bf16[8,72,128]{2,1,0:T(8,128)(2,1)S(1)} %get-tuple-element.17), channel_id=1, replica_groups={{0,2,4,6,8,10,12,14},{1,3,5,7,9,11,13,15},{16,18,20,22,24,26,28,30},{17..., dimensions={0} | all-to-all | bytes 294912 | tf_op jit(solution)/shard_map/all_to_all | solution.py:210
  53.3 0.0 copy-start.2
  53.3 0.0 collective-permute-done
  53.4 0.1 constant_dynamic-update-slice_fusion
  53.5 2.1 %collective-permute-start.1 = (bf16[4608,128]{1,0:T(8,128)(2,1)S(1)}, bf16[4608,128]{1,0:T(8,128)(2,1)S(1)}, u32[]{:S(2)}, u32[]{:S(2)}) collective-permute-start(bf16[4608,128]{1,0:T(8,128)(2,1)S(1)} %constant_dynamic-update-slice_fusion), channel_id=1, source_target_pairs={{0,8},{8,0},{16,24},{24,16},{32,40},{40,32},{48,56},{56,48},{64,72... | collective-permute-start | bytes 3538952 | tf_op jit(solution)/shard_map/ppermute | solution.py:215
  55.6 4.7 %collective-permute-start.2 = (bf16[8,72,128]{2,1,0:T(8,128)(2,1)S(1)}, bf16[8,72,128]{2,1,0:T(8,128)(2,1)S(1)}, u32[]{:S(2)}, u32[]{:S(2)}) collective-permute-start(bf16[8,72,128]{2,1,0:T(8,128)(2,1)S(1)} %all_to_all.10.rows_ref), channel_id=1, source_target_pairs={{0,1},{1,0},{2,3},{3,2},{4,5},{5,4},{6,7},{7,6},{8,9},{9,8},{10,11... | collective-permute-start | bytes 442376 | tf_op jit(solution)/shard_map/ppermute | solution.py:212
  60.3 0.0 collective-permute-done.1
  60.3 0.0 copy-done.2
  60.3 0.0 copy-start
  60.3 4.0 %shard_map.47 = bf16[192,384]{1,0:T(8,128)(2,1)S(1)} custom-call(s32[64]{0:T(128)S(1)} %copy-done.2, bf16[2,16,144,128]{3,2,1,0:T(8,128)(2,1)S(1)} %bitcast.7, bf16[2,16,144,128]{3,2,1,0:T(8,128)(2,1)S(1)} %bitcast.8, bf16[4,96,6144]{2,1,0:T(8,128)(2,1)} %integrals_ref.1), custom_call_target="tpu_custom_call" | custom-call | tf_op jit(solution)/shard_map/pallas_call | solution.py:188
  64.3 2.0 %all-gather = bf16[384,384]{1,0:T(8,128)(2,1)S(1)} all-gather(bf16[192,384]{1,0:T(8,128)(2,1)S(1)} %shard_map.47), channel_id=2, replica_groups={{0,8},{16,24},{32,40},{48,56},{64,72},{80,88},{96,104},{112,120},{128,1..., dimensions={0}, use_global_device_ids=true | all-gather | bytes 442368 | tf_op jit(solution)/shard_map/all_gather | solution.py:224
  66.3 0.0 collective-permute-done.2.far_rows_ref
  66.3 0.0 copy-done
  66.3 1.4 %shard_map.48 = (f32[8,72,128]{2,1,0:T(8,128)S(1)}, bf16[8,72,128]{2,1,0:T(8,128)(2,1)S(1)}) custom-call(bf16[2,192,384]{2,1,0:T(8,128)(2,1)S(1)} %bitcast.9, bf16[8,72,128]{2,1,0:T(8,128)(2,1)S(1)} %all_to_all.10.rows_ref, bf16[8,72,128]{2,1,0:T(8,128)(2,1)S(1)} %collective-permute-done.2.far_rows_ref, bf16[384,96]{1,0:T(8,128)(2,1)S(1)} %copy-done), custom_call_target="tpu_custom_call" | custom-call | tf_op jit(solution)/shard_map/pallas_call | solution.py:188
  67.7 6.6 %all-gather.1 = bf16[16,72,128]{2,1,0:T(8,128)(2,1)S(1)} all-gather(bf16[8,72,128]{2,1,0:T(8,128)(2,1)S(1)} %get-tuple-element.22), channel_id=3, replica_groups={{0,16},{8,24},{32,48},{40,56},{64,80},{72,88},{96,112},{104,120},{128,1..., dimensions={0}, use_global_device_ids=true | all-gather | bytes 442368 | tf_op jit(solution)/shard_map/all_gather | solution.py:229
  74.4 22.1 %all_to_all.11.terms_ref = bf16[16,40,128]{2,1,0:T(8,128)(2,1)S(1)} all-to-all(bf16[16,40,128]{2,1,0:T(8,128)(2,1)S(1)} %shard_map.49), channel_id=1, replica_groups={{0,32,64,96,128,160,192,224,256,288,320,352,384,416,448,480},{8,40,72,1..., dimensions={0} | all-to-all | bytes 327680 | tf_op jit(solution)/shard_map/all_to_all | solution.py:231
  96.4 4.5 %all-gather.2 = f32[80,128]{1,0:T(8,128)S(1)} all-gather(f32[40,128]{1,0:T(8,128)S(1)} %shard_map.50), channel_id=4, replica_groups={{0,32},{8,40},{16,48},{24,56},{64,96},{72,104},{80,112},{88,120},{128,1..., dimensions={0}, use_global_device_ids=true | all-gather | bytes 61440 | tf_op jit(solution)/shard_map/all_gather | solution.py:233
  100.9 0.8 shard_map.51
  (3 shorter events, 0.1 us)
Async XLA Ops:
  0.0 0.8 copy-start.1
  40.0 13.3 %collective-permute-start = (bf16[2304,128]{1,0:T(8,128)(2,1)S(1)}, bf16[2304,128]{1,0:T(8,128)(2,1)S(1)}, u32[]{:S(2)}, u32[]{:S(2)}) collective-permute-start(bf16[2304,128]{1,0:T(8,128)(2,1)S(1)} %all_gather.25), channel_id=1, source_target_pairs={{0,16},{8,24},{16,0},{24,8},{32,48},{40,56},{48,32},{56,40},{64,80... | collective-permute-start | bytes 1769480 | tf_op jit(solution)/shard_map/ppermute | solution.py:209
  53.3 6.9 %copy-start.2 = (s32[64]{0:T(128)S(1)}, s32[64]{0:T(128)}, u32[]{:S(2)}) copy-start(s32[64]{0:T(128)} %live_ref.1) | copy-start | bytes 772
  53.5 6.8 %collective-permute-start.1 = (bf16[4608,128]{1,0:T(8,128)(2,1)S(1)}, bf16[4608,128]{1,0:T(8,128)(2,1)S(1)}, u32[]{:S(2)}, u32[]{:S(2)}) collective-permute-start(bf16[4608,128]{1,0:T(8,128)(2,1)S(1)} %constant_dynamic-update-slice_fusion), channel_id=1, source_target_pairs={{0,8},{8,0},{16,24},{24,16},{32,40},{40,32},{48,56},{56,48},{64,72... | collective-permute-start | bytes 3538952 | tf_op jit(solution)/shard_map/ppermute | solution.py:215
  55.6 10.7 %collective-permute-start.2 = (bf16[8,72,128]{2,1,0:T(8,128)(2,1)S(1)}, bf16[8,72,128]{2,1,0:T(8,128)(2,1)S(1)}, u32[]{:S(2)}, u32[]{:S(2)}) collective-permute-start(bf16[8,72,128]{2,1,0:T(8,128)(2,1)S(1)} %all_to_all.10.rows_ref), channel_id=1, source_target_pairs={{0,1},{1,0},{2,3},{3,2},{4,5},{5,4},{6,7},{7,6},{8,9},{9,8},{10,11... | collective-permute-start | bytes 442376 | tf_op jit(solution)/shard_map/ppermute | solution.py:212
  60.3 6.0 %copy-start = (bf16[384,96]{1,0:T(8,128)(2,1)S(1)}, bf16[384,96]{1,0:T(8,128)(2,1)}, u32[]{:S(2)}) copy-start(bf16[384,96]{1,0:T(8,128)(2,1)} %constant.2.clone.signs_ref) | copy-start | bytes 221188

commit v7 on v6

--- a/solution.py
+++ b/solution.py
@@ -125,16 +125,16 @@
     return jnp.concatenate([block[: 4 * J, :S], jnp.concatenate([block[: 4 * J, S:], low], axis=1)], axis=0)
 
 
+def weights_of(rows_ref, y, signs_ref):
+    rows = jnp.concatenate([rows_of(rows_ref[4 * core + y]) for core in range(2)], axis=1).astype(jnp.bfloat16)
+    return jnp.dot(signs_ref[...], rows, preferred_element_type=jnp.float32).astype(jnp.bfloat16)
+
+
 def term_kernel(half_ref, rows_ref, far_rows_ref, signs_ref, keep_ref, give_ref):
     x = lax.axis_index("pair") % Q // 2
     side = lax.axis_index("spin") % 2
     half = [jnp.concatenate([half_ref[core, :, c * S : (c + 1) * S] for core in range(2)], axis=1) for c in range(4)]
-    signed = []
-    for e in range(SPIN):
-        groups = [4 * core + e // 2 for core in range(2)]
-        rows = [rows_of(jnp.where(side == e % 2, rows_ref[g], far_rows_ref[g])) for g in groups]
-        rows = jnp.concatenate(rows, axis=1).astype(jnp.bfloat16)
-        signed.append(jnp.dot(signs_ref[...], rows, preferred_element_type=jnp.float32).astype(jnp.bfloat16))
+    signed = [weights_of(ref, y, signs_ref) for ref in (rows_ref, far_rows_ref) for y in range(4)]
     terms = []
     for column in range(2):
         term = None
@@ -147,7 +147,8 @@
         for e in range(SPIN):
             part = term[e * 4 * J : (e + 1) * 4 * J]
             tail = jnp.concatenate([part[: 2 * J, 128:], part[2 * J :, 128:]], axis=1)
-            ref[e] = jnp.concatenate([part[:, :128], tail], axis=0).astype(ref.dtype)
+            block = 2 * (e % 4) + (side if e < 4 else 1 - side)
+            ref[block] = jnp.concatenate([part[:, :128], tail], axis=0).astype(ref.dtype)
 
 
 def join_kernel(keep_ref, given_ref, out_ref):

time: 102 us -> 102 us (level)
  no operation moved by 1% of the time
where the time goes in v7:
time: 102 us
  blocking collectives  84 us (82%)
  starting transfers between devices  10.2 us (10%)
  Pallas kernels  6.5 us (6%)
    all_gather x1, blocking collectives, shards(): line = lax.all_gather(packed, 'pair', axis_index_groups=FAR, tiled=True)  25 us
    all_to_all x1, blocking collectives, shards(): terms = lax.all_to_all(terms, 'pair', 0, 0, axis_index_groups=LINE)  22 us
    all_gather x1, blocking collectives, shards(): line = lax.all_gather(line, 'pair', axis_index_groups=NEAR, tiled=True)  14 us
    all_to_all x1, blocking collectives, shards(): rows = lax.all_to_all(rows, ('pair', 'spin'), 0, 0, axis_index_groups=ROWS)  9.9 us
    all_gather x1, blocking collectives, shards(): given = lax.all_gather(give, 'pair', axis_index_groups=ACROSS)  6.58 us
    pallas_call x6, Pallas kernels, run(): pl.pallas_call(kernel, out_shape=out_shape, in_specs=in_specs or [vmem] *...  6.5 us
    ppermute x1, starting transfers between devices, shards(): far_rows = lax.ppermute(rows, 'spin', swap(1, SPIN))  4.65 us
    all_gather x1, blocking collectives, shards(): sums = lax.all_gather(sums, 'pair', axis_index_groups=PLANE_PAIRS)  4.46 us
  transfers between devices with their start and end apart: 3, of which 0 were waited for; matrix products, arithmetic and copies ran while one was open for 0% of the time, Pallas kernels for 4%

profile of v7, /device:TPU:32, one launch (start us, length us, event | category | flops | bytes accessed | tf_op | source)
XLA Modules:
  0.0 101.7 jit_solution(10835680287683317717)
XLA Ops:
  0.0 0.0 copy-start.1
  0.0 0.8 copy-done.1
  0.8 0.2 shard_map.46
  1.1 25.0 %all_gather.24 = bf16[576,128]{1,0:T(8,128)(2,1)S(1)} all-gather(bf16[144,128]{1,0:T(8,128)(2,1)S(1)} %get-tuple-element.14), channel_id=1, replica_groups={{0,128,256,384},{8,136,264,392},{16,144,272,400},{24,152,280,408},{32,1..., dimensions={0}, use_global_device_ids=true | all-gather | bytes 184320 | tf_op jit(solution)/shard_map/all_gather | solution.py:207
  26.0 14.0 %all_gather.25 = bf16[2304,128]{1,0:T(8,128)(2,1)S(1)} all-gather(bf16[576,128]{1,0:T(8,128)(2,1)S(1)} %all_gather.24), channel_id=1, replica_groups={{0,32,96,64},{8,40,104,72},{16,48,112,80},{24,56,120,88},{128,160,224,1..., dimensions={0}, use_global_device_ids=true | all-gather | bytes 737280 | tf_op jit(solution)/shard_map/all_gather | solution.py:208
  40.0 3.4 %collective-permute-start = (bf16[2304,128]{1,0:T(8,128)(2,1)S(1)}, bf16[2304,128]{1,0:T(8,128)(2,1)S(1)}, u32[]{:S(2)}, u32[]{:S(2)}) collective-permute-start(bf16[2304,128]{1,0:T(8,128)(2,1)S(1)} %all_gather.25), channel_id=1, source_target_pairs={{0,16},{8,24},{16,0},{24,8},{32,48},{40,56},{48,32},{56,40},{64,80... | collective-permute-start | bytes 1769480 | tf_op jit(solution)/shard_map/ppermute | solution.py:210
  43.4 9.9 %all_to_all.10.rows_ref = bf16[8,72,128]{2,1,0:T(8,128)(2,1)S(1)} all-to-all(bf16[8,72,128]{2,1,0:T(8,128)(2,1)S(1)} %get-tuple-element.17), channel_id=1, replica_groups={{0,2,4,6,8,10,12,14},{1,3,5,7,9,11,13,15},{16,18,20,22,24,26,28,30},{17..., dimensions={0} | all-to-all | bytes 294912 | tf_op jit(solution)/shard_map/all_to_all | solution.py:211
  53.3 0.0 copy-start.2
  53.3 0.0 collective-permute-done
  53.4 0.1 constant_dynamic-update-slice_fusion
  53.5 2.1 %collective-permute-start.1 = (bf16[4608,128]{1,0:T(8,128)(2,1)S(1)}, bf16[4608,128]{1,0:T(8,128)(2,1)S(1)}, u32[]{:S(2)}, u32[]{:S(2)}) collective-permute-start(bf16[4608,128]{1,0:T(8,128)(2,1)S(1)} %constant_dynamic-update-slice_fusion), channel_id=1, source_target_pairs={{0,8},{8,0},{16,24},{24,16},{32,40},{40,32},{48,56},{56,48},{64,72... | collective-permute-start | bytes 3538952 | tf_op jit(solution)/shard_map/ppermute | solution.py:216
  55.6 4.7 %collective-permute-start.2 = (bf16[8,72,128]{2,1,0:T(8,128)(2,1)S(1)}, bf16[8,72,128]{2,1,0:T(8,128)(2,1)S(1)}, u32[]{:S(2)}, u32[]{:S(2)}) collective-permute-start(bf16[8,72,128]{2,1,0:T(8,128)(2,1)S(1)} %all_to_all.10.rows_ref), channel_id=1, source_target_pairs={{0,1},{1,0},{2,3},{3,2},{4,5},{5,4},{6,7},{7,6},{8,9},{9,8},{10,11... | collective-permute-start | bytes 442376 | tf_op jit(solution)/shard_map/ppermute | solution.py:213
  60.3 0.0 collective-permute-done.1
  60.3 0.0 copy-done.2
  60.3 0.0 copy-start
  60.3 4.0 %shard_map.47 = bf16[192,384]{1,0:T(8,128)(2,1)S(1)} custom-call(s32[64]{0:T(128)S(1)} %copy-done.2, bf16[2,16,144,128]{3,2,1,0:T(8,128)(2,1)S(1)} %bitcast.7, bf16[2,16,144,128]{3,2,1,0:T(8,128)(2,1)S(1)} %bitcast.8, bf16[4,96,6144]{2,1,0:T(8,128)(2,1)} %integrals_ref.1), custom_call_target="tpu_custom_call" | custom-call | tf_op jit(solution)/shard_map/pallas_call | solution.py:189
  64.3 2.0 %all-gather = bf16[384,384]{1,0:T(8,128)(2,1)S(1)} all-gather(bf16[192,384]{1,0:T(8,128)(2,1)S(1)} %shard_map.47), channel_id=2, replica_groups={{0,8},{16,24},{32,40},{48,56},{64,72},{80,88},{96,104},{112,120},{128,1..., dimensions={0}, use_global_device_ids=true | all-gather | bytes 442368 | tf_op jit(solution)/shard_map/all_gather | solution.py:225
  66.3 0.0 collective-permute-done.2.far_rows_ref
  66.3 0.0 copy-done
  66.3 1.4 %shard_map.48 = (f32[8,72,128]{2,1,0:T(8,128)S(1)}, bf16[8,72,128]{2,1,0:T(8,128)(2,1)S(1)}) custom-call(bf16[2,192,384]{2,1,0:T(8,128)(2,1)S(1)} %bitcast.9, bf16[8,72,128]{2,1,0:T(8,128)(2,1)S(1)} %all_to_all.10.rows_ref, bf16[8,72,128]{2,1,0:T(8,128)(2,1)S(1)} %collective-permute-done.2.far_rows_ref, bf16[384,96]{1,0:T(8,128)(2,1)S(1)} %copy-done), custom_call_target="tpu_custom_call" | custom-call | tf_op jit(solution)/shard_map/pallas_call | solution.py:189
  67.7 6.6 %all-gather.1 = bf16[16,72,128]{2,1,0:T(8,128)(2,1)S(1)} all-gather(bf16[8,72,128]{2,1,0:T(8,128)(2,1)S(1)} %get-tuple-element.22), channel_id=3, replica_groups={{0,16},{8,24},{32,48},{40,56},{64,80},{72,88},{96,112},{104,120},{128,1..., dimensions={0}, use_global_device_ids=true | all-gather | bytes 442368 | tf_op jit(solution)/shard_map/all_gather | solution.py:230
  74.3 22.0 %all_to_all.11.terms_ref = bf16[16,40,128]{2,1,0:T(8,128)(2,1)S(1)} all-to-all(bf16[16,40,128]{2,1,0:T(8,128)(2,1)S(1)} %shard_map.49), channel_id=1, replica_groups={{0,32,64,96,128,160,192,224,256,288,320,352,384,416,448,480},{8,40,72,1..., dimensions={0} | all-to-all | bytes 327680 | tf_op jit(solution)/shard_map/all_to_all | solution.py:232
  96.4 4.5 %all-gather.2 = f32[80,128]{1,0:T(8,128)S(1)} all-gather(f32[40,128]{1,0:T(8,128)S(1)} %shard_map.50), channel_id=4, replica_groups={{0,32},{8,40},{16,48},{24,56},{64,96},{72,104},{80,112},{88,120},{128,1..., dimensions={0}, use_global_device_ids=true | all-gather | bytes 61440 | tf_op jit(solution)/shard_map/all_gather | solution.py:234
  100.9 0.8 shard_map.51
  (3 shorter events, 0.1 us)
Async XLA Ops:
  0.0 0.8 copy-start.1
  40.0 13.3 %collective-permute-start = (bf16[2304,128]{1,0:T(8,128)(2,1)S(1)}, bf16[2304,128]{1,0:T(8,128)(2,1)S(1)}, u32[]{:S(2)}, u32[]{:S(2)}) collective-permute-start(bf16[2304,128]{1,0:T(8,128)(2,1)S(1)} %all_gather.25), channel_id=1, source_target_pairs={{0,16},{8,24},{16,0},{24,8},{32,48},{40,56},{48,32},{56,40},{64,80... | collective-permute-start | bytes 1769480 | tf_op jit(solution)/shard_map/ppermute | solution.py:210
  53.3 6.9 %copy-start.2 = (s32[64]{0:T(128)S(1)}, s32[64]{0:T(128)}, u32[]{:S(2)}) copy-start(s32[64]{0:T(128)} %live_ref.1) | copy-start | bytes 772
  53.5 6.8 %collective-permute-start.1 = (bf16[4608,128]{1,0:T(8,128)(2,1)S(1)}, bf16[4608,128]{1,0:T(8,128)(2,1)S(1)}, u32[]{:S(2)}, u32[]{:S(2)}) collective-permute-start(bf16[4608,128]{1,0:T(8,128)(2,1)S(1)} %constant_dynamic-update-slice_fusion), channel_id=1, source_target_pairs={{0,8},{8,0},{16,24},{24,16},{32,40},{40,32},{48,56},{56,48},{64,72... | collective-permute-start | bytes 3538952 | tf_op jit(solution)/shard_map/ppermute | solution.py:216
  55.6 10.7 %collective-permute-start.2 = (bf16[8,72,128]{2,1,0:T(8,128)(2,1)S(1)}, bf16[8,72,128]{2,1,0:T(8,128)(2,1)S(1)}, u32[]{:S(2)}, u32[]{:S(2)}) collective-permute-start(bf16[8,72,128]{2,1,0:T(8,128)(2,1)S(1)} %all_to_all.10.rows_ref), channel_id=1, source_target_pairs={{0,1},{1,0},{2,3},{3,2},{4,5},{5,4},{6,7},{7,6},{8,9},{9,8},{10,11... | collective-permute-start | bytes 442376 | tf_op jit(solution)/shard_map/ppermute | solution.py:213
  60.3 6.0 %copy-start = (bf16[384,96]{1,0:T(8,128)(2,1)S(1)}, bf16[384,96]{1,0:T(8,128)(2,1)}, u32[]{:S(2)}) copy-start(bf16[384,96]{1,0:T(8,128)(2,1)} %constant.2.clone.signs_ref) | copy-start | bytes 221188

commit v8 on v7

--- a/solution.py
+++ b/solution.py
@@ -218,7 +218,7 @@
         half_kernel,
         shape((PQ * K, 4 * S), bf16),
         [pl.BlockSpec(memory_space=pltpu.SMEM), vmem, vmem, pl.BlockSpec((PQ, S, PLANES * PLANE // 2), lambda i: (0, 0, i))],
-        50,
+        24,
         grid=(2,),
         scratch_shapes=[pltpu.VMEM((CK, PQ * S), jnp.float32)],
     )(live, own.reshape(2, PLANES, PACKED, 128), other.reshape(2, PLANES, PACKED, 128), integrals)

time: 102 us -> 103 us (level)
  local copies, waits for them, and re-layouts: 0.93 us -> 3.26 us
    unnamed x7 -> x9, local copies, waits for them, and re-layouts: 0.85 us -> 3.18 us
  transfers between devices with their start and end apart: 3 -> 3, of which waited for: 0 -> 0; matrix products, arithmetic and copies ran while one was open for 0% -> 0% of each run, Pallas kernels for 4% -> 3%
where the time goes in v8:
time: 103 us
  blocking collectives  84 us (82%)
  starting transfers between devices  10.2 us (10%)
  Pallas kernels  5.49 us (5%)
  local copies, waits for them, and re-layouts  3.26 us (3%)
    all_gather x1, blocking collectives, shards(): line = lax.all_gather(packed, 'pair', axis_index_groups=FAR, tiled=True)  25 us
    all_to_all x1, blocking collectives, shards(): terms = lax.all_to_all(terms, 'pair', 0, 0, axis_index_groups=LINE)  22.1 us
    all_gather x1, blocking collectives, shards(): line = lax.all_gather(line, 'pair', axis_index_groups=NEAR, tiled=True)  14 us
    all_to_all x1, blocking collectives, shards(): rows = lax.all_to_all(rows, ('pair', 'spin'), 0, 0, axis_index_groups=ROWS)  9.9 us
    all_gather x1, blocking collectives, shards(): given = lax.all_gather(give, 'pair', axis_index_groups=ACROSS)  6.58 us
    pallas_call x6, Pallas kernels, run(): pl.pallas_call(kernel, out_shape=out_shape, in_specs=in_specs or [vmem] *...  5.49 us
    ppermute x1, starting transfers between devices, shards(): far_rows = lax.ppermute(rows, 'spin', swap(1, SPIN))  4.65 us
    all_gather x1, blocking collectives, shards(): sums = lax.all_gather(sums, 'pair', axis_index_groups=PLANE_PAIRS)  4.46 us
  transfers between devices with their start and end apart: 3, of which 0 were waited for; matrix products, arithmetic and copies ran while one was open for 0% of the time, Pallas kernels for 3%

profile of v8, /device:TPU:32, one launch (start us, length us, event | category | flops | bytes accessed | tf_op | source)
XLA Modules:
  0.0 103.0 jit_solution(2767775799045778750)
XLA Ops:
  0.0 0.0 copy-start.2
  0.0 0.8 copy-done.2
  0.8 0.2 shard_map.46
  1.1 25.0 %all_gather.24 = bf16[576,128]{1,0:T(8,128)(2,1)S(1)} all-gather(bf16[144,128]{1,0:T(8,128)(2,1)S(1)} %get-tuple-element.14), channel_id=1, replica_groups={{0,128,256,384},{8,136,264,392},{16,144,272,400},{24,152,280,408},{32,1..., dimensions={0}, use_global_device_ids=true | all-gather | bytes 184320 | tf_op jit(solution)/shard_map/all_gather | solution.py:207
  26.0 14.0 %all_gather.25 = bf16[2304,128]{1,0:T(8,128)(2,1)S(1)} all-gather(bf16[576,128]{1,0:T(8,128)(2,1)S(1)} %all_gather.24), channel_id=1, replica_groups={{0,32,96,64},{8,40,104,72},{16,48,112,80},{24,56,120,88},{128,160,224,1..., dimensions={0}, use_global_device_ids=true | all-gather | bytes 737280 | tf_op jit(solution)/shard_map/all_gather | solution.py:208
  40.0 3.4 %collective-permute-start = (bf16[2304,128]{1,0:T(8,128)(2,1)S(1)}, bf16[2304,128]{1,0:T(8,128)(2,1)S(1)}, u32[]{:S(2)}, u32[]{:S(2)}) collective-permute-start(bf16[2304,128]{1,0:T(8,128)(2,1)S(1)} %all_gather.25), channel_id=1, source_target_pairs={{0,16},{8,24},{16,0},{24,8},{32,48},{40,56},{48,32},{56,40},{64,80... | collective-permute-start | bytes 1769480 | tf_op jit(solution)/shard_map/ppermute | solution.py:210
  43.4 9.9 %all_to_all.10.rows_ref = bf16[8,72,128]{2,1,0:T(8,128)(2,1)S(1)} all-to-all(bf16[8,72,128]{2,1,0:T(8,128)(2,1)S(1)} %get-tuple-element.17), channel_id=1, replica_groups={{0,2,4,6,8,10,12,14},{1,3,5,7,9,11,13,15},{16,18,20,22,24,26,28,30},{17..., dimensions={0} | all-to-all | bytes 294912 | tf_op jit(solution)/shard_map/all_to_all | solution.py:211
  53.3 0.0 copy-start.3
  53.3 0.0 collective-permute-done
  53.4 0.1 constant_dynamic-update-slice_fusion
  53.5 2.1 %collective-permute-start.1 = (bf16[4608,128]{1,0:T(8,128)(2,1)S(1)}, bf16[4608,128]{1,0:T(8,128)(2,1)S(1)}, u32[]{:S(2)}, u32[]{:S(2)}) collective-permute-start(bf16[4608,128]{1,0:T(8,128)(2,1)S(1)} %constant_dynamic-update-slice_fusion), channel_id=1, source_target_pairs={{0,8},{8,0},{16,24},{24,16},{32,40},{40,32},{48,56},{56,48},{64,72... | collective-permute-start | bytes 3538952 | tf_op jit(solution)/shard_map/ppermute | solution.py:216
  55.6 4.7 %collective-permute-start.2 = (bf16[8,72,128]{2,1,0:T(8,128)(2,1)S(1)}, bf16[8,72,128]{2,1,0:T(8,128)(2,1)S(1)}, u32[]{:S(2)}, u32[]{:S(2)}) collective-permute-start(bf16[8,72,128]{2,1,0:T(8,128)(2,1)S(1)} %all_to_all.10.rows_ref), channel_id=1, source_target_pairs={{0,1},{1,0},{2,3},{3,2},{4,5},{5,4},{6,7},{7,6},{8,9},{9,8},{10,11... | collective-permute-start | bytes 442376 | tf_op jit(solution)/shard_map/ppermute | solution.py:213
  60.3 0.0 collective-permute-done.1
  60.3 0.0 copy-done.3
  60.3 0.0 copy-start
  60.3 2.3 %copy-done = bf16[4,96,6144]{2,1,0:T(8,128)(2,1)S(1)} copy-done((bf16[4,96,6144]{2,1,0:T(8,128)(2,1)S(1)}, bf16[4,96,6144]{2,1,0:T(8,128)(2,1)}, u32[]{:S(2)}) %copy-start) | copy-done | bytes 4718616
  62.6 0.0 copy-start.1
  62.6 3.0 %shard_map.47 = bf16[192,384]{1,0:T(8,128)(2,1)S(1)} custom-call(s32[64]{0:T(128)S(1)} %copy-done.3, bf16[2,16,144,128]{3,2,1,0:T(8,128)(2,1)S(1)} %bitcast.7, bf16[2,16,144,128]{3,2,1,0:T(8,128)(2,1)S(1)} %bitcast.8, bf16[4,96,6144]{2,1,0:T(8,128)(2,1)S(1)} %copy-done), custom_call_target="tpu_custom_call" | custom-call | tf_op jit(solution)/shard_map/pallas_call | solution.py:189
  65.6 2.0 %all-gather = bf16[384,384]{1,0:T(8,128)(2,1)S(1)} all-gather(bf16[192,384]{1,0:T(8,128)(2,1)S(1)} %shard_map.47), channel_id=2, replica_groups={{0,8},{16,24},{32,40},{48,56},{64,72},{80,88},{96,104},{112,120},{128,1..., dimensions={0}, use_global_device_ids=true | all-gather | bytes 442368 | tf_op jit(solution)/shard_map/all_gather | solution.py:225
  67.6 0.0 collective-permute-done.2.far_rows_ref
  67.6 0.0 copy-done.1
  67.6 1.4 %shard_map.48 = (f32[8,72,128]{2,1,0:T(8,128)S(1)}, bf16[8,72,128]{2,1,0:T(8,128)(2,1)S(1)}) custom-call(bf16[2,192,384]{2,1,0:T(8,128)(2,1)S(1)} %bitcast.9, bf16[8,72,128]{2,1,0:T(8,128)(2,1)S(1)} %all_to_all.10.rows_ref, bf16[8,72,128]{2,1,0:T(8,128)(2,1)S(1)} %collective-permute-done.2.far_rows_ref, bf16[384,96]{1,0:T(8,128)(2,1)S(1)} %copy-done.1), custom_call_target="tpu_custom_call" | custom-call | tf_op jit(solution)/shard_map/pallas_call | solution.py:189
  69.0 6.6 %all-gather.1 = bf16[16,72,128]{2,1,0:T(8,128)(2,1)S(1)} all-gather(bf16[8,72,128]{2,1,0:T(8,128)(2,1)S(1)} %get-tuple-element.22), channel_id=3, replica_groups={{0,16},{8,24},{32,48},{40,56},{64,80},{72,88},{96,112},{104,120},{128,1..., dimensions={0}, use_global_device_ids=true | all-gather | bytes 442368 | tf_op jit(solution)/shard_map/all_gather | solution.py:230
  75.7 22.1 %all_to_all.11.terms_ref = bf16[16,40,128]{2,1,0:T(8,128)(2,1)S(1)} all-to-all(bf16[16,40,128]{2,1,0:T(8,128)(2,1)S(1)} %shard_map.49), channel_id=1, replica_groups={{0,32,64,96,128,160,192,224,256,288,320,352,384,416,448,480},{8,40,72,1..., dimensions={0} | all-to-all | bytes 327680 | tf_op jit(solution)/shard_map/all_to_all | solution.py:232
  97.7 4.5 %all-gather.2 = f32[80,128]{1,0:T(8,128)S(1)} all-gather(f32[40,128]{1,0:T(8,128)S(1)} %shard_map.50), channel_id=4, replica_groups={{0,32},{8,40},{16,48},{24,56},{64,96},{72,104},{80,112},{88,120},{128,1..., dimensions={0}, use_global_device_ids=true | all-gather | bytes 61440 | tf_op jit(solution)/shard_map/all_gather | solution.py:234
  102.2 0.8 shard_map.51
  (3 shorter events, 0.1 us)
Async XLA Ops:
  0.0 0.8 copy-start.2
  40.0 13.3 %collective-permute-start = (bf16[2304,128]{1,0:T(8,128)(2,1)S(1)}, bf16[2304,128]{1,0:T(8,128)(2,1)S(1)}, u32[]{:S(2)}, u32[]{:S(2)}) collective-permute-start(bf16[2304,128]{1,0:T(8,128)(2,1)S(1)} %all_gather.25), channel_id=1, source_target_pairs={{0,16},{8,24},{16,0},{24,8},{32,48},{40,56},{48,32},{56,40},{64,80... | collective-permute-start | bytes 1769480 | tf_op jit(solution)/shard_map/ppermute | solution.py:210
  53.3 6.9 %copy-start.3 = (s32[64]{0:T(128)S(1)}, s32[64]{0:T(128)}, u32[]{:S(2)}) copy-start(s32[64]{0:T(128)} %live_ref.1) | copy-start | bytes 772
  53.5 6.8 %collective-permute-start.1 = (bf16[4608,128]{1,0:T(8,128)(2,1)S(1)}, bf16[4608,128]{1,0:T(8,128)(2,1)S(1)}, u32[]{:S(2)}, u32[]{:S(2)}) collective-permute-start(bf16[4608,128]{1,0:T(8,128)(2,1)S(1)} %constant_dynamic-update-slice_fusion), channel_id=1, source_target_pairs={{0,8},{8,0},{16,24},{24,16},{32,40},{40,32},{48,56},{56,48},{64,72... | collective-permute-start | bytes 3538952 | tf_op jit(solution)/shard_map/ppermute | solution.py:216
  55.6 12.0 %collective-permute-start.2 = (bf16[8,72,128]{2,1,0:T(8,128)(2,1)S(1)}, bf16[8,72,128]{2,1,0:T(8,128)(2,1)S(1)}, u32[]{:S(2)}, u32[]{:S(2)}) collective-permute-start(bf16[8,72,128]{2,1,0:T(8,128)(2,1)S(1)} %all_to_all.10.rows_ref), channel_id=1, source_target_pairs={{0,1},{1,0},{2,3},{3,2},{4,5},{5,4},{6,7},{7,6},{8,9},{9,8},{10,11... | collective-permute-start | bytes 442376 | tf_op jit(solution)/shard_map/ppermute | solution.py:213
  60.3 2.3 %copy-start = (bf16[4,96,6144]{2,1,0:T(8,128)(2,1)S(1)}, bf16[4,96,6144]{2,1,0:T(8,128)(2,1)}, u32[]{:S(2)}) copy-start(bf16[4,96,6144]{2,1,0:T(8,128)(2,1)} %integrals_ref.1) | copy-start | bytes 14155780
  62.6 5.0 %copy-start.1 = (bf16[384,96]{1,0:T(8,128)(2,1)S(1)}, bf16[384,96]{1,0:T(8,128)(2,1)}, u32[]{:S(2)}) copy-start(bf16[384,96]{1,0:T(8,128)(2,1)} %constant.2.clone.signs_ref) | copy-start | bytes 221188
